TPU v7x, 32 devices: a whole 2x2x4 slice. The times are simulated.
32 devices in a mesh: sub: 8 (over y, x, core), grp: 4 (over z).
Axes of the slice: x: 2, y: 2, z: 4, core: 2. Of those that a mesh axis runs over, the one named last changes fastest.
Arguments:
- phi: bfloat16 [64, 400, 2048], P('sub', 'grp'), may hold values from -0.5 to 0.5
- psi: bfloat16 [64, 400, 2048], P('sub', 'grp'), may hold values from -1.25 to 1.25
- k_blocks: bfloat16 [64, 24, 128, 128], P('sub'), may hold values from -0.5 to 0.5
- m_blocks: bfloat16 [64, 24, 128, 128], P('sub'), may hold values from -0.5 to 0.5
- block_row: int32 [64, 24], P('sub'), may hold values from 0 to 15
- block_col: int32 [64, 24], P('sub'), may hold values from 0 to 31
- live: int32 [64], P('sub'), may hold values from 1 to 24, 768 in all
Outputs:
- grid_k: float32 [8, 4, 8, 100, 800], P('sub', 'grp')
- grid_m: float32 [8, 4, 8, 100, 800], P('sub', 'grp')
Inputs may be any that keep to these rules, and one draw needn't show every extreme that they name: Slots n >= live[i] are not part of substructure i's pattern; the largest count is 24. `block_row`: several used slots may name the same block position; their terms add. `block_col`: blocks below 16 lie on the left interface, the others on the right one.
All inputs are finite; a program needn't handle non-finite values. No bound on the sum of `live` on one device may be relied on, other than what follows from the above.
Results may differ from a plain program's by a relative error of at most 0.0029.
Values may be sent and summed in bfloat16 or wider, within the bound.
No kernel may reach another device: no remote copies, remote signals or barrier semaphores. Data moves between devices by JAX's collectives and lax.ppermute only.
A program may use at most 256 MiB of HBM per device.

v0:
```python
import jax
import jax.numpy as jnp
from jax import lax
from jax.sharding import PartitionSpec as P


def passed_along(shard, axis, by):
    length = lax.axis_size(axis)
    pairs = [(i, i + by) for i in range(length) if 0 <= i + by < length]
    return lax.ppermute(shard, axis, pairs)


def per_device(phi, psi, k_blocks, m_blocks, block_row, block_col, live):
    count, quarter, width = phi.shape
    slots = k_blocks.shape[1]
    edge = k_blocks.shape[2]
    blocks_per = width // edge
    right_modes = lax.all_gather(psi, "grp", axis=1, tiled=True)
    border = passed_along(right_modes[count - 1], "sub", 1)
    left_modes = jnp.concatenate([border[None], right_modes[:-1]], axis=0)
    modes = right_modes.shape[1]
    slot_ids = jnp.arange(slots, dtype=jnp.int32)
    used = slot_ids[None, :] < live[:, None]
    row_hot = (
        (block_row[:, :, None] == jnp.arange(blocks_per, dtype=jnp.int32)) & used[:, :, None]
    ).astype(jnp.bfloat16)
    col_hot = (block_col[:, :, None] == jnp.arange(2 * blocks_per, dtype=jnp.int32)).astype(
        jnp.float32
    )
    phi_blocks = phi.reshape(count, quarter, blocks_per, edge)
    picked = jnp.einsum(
        "snb,sqbc->snqc", row_hot, phi_blocks, preferred_element_type=jnp.float32
    ).astype(jnp.bfloat16)

    def couple_one(blocks):
        term = jnp.einsum("snqc,sncd->snqd", picked, blocks, preferred_element_type=jnp.float32)
        placed = jnp.einsum("snqd,snb->sqbd", term, col_hot, precision=lax.Precision.HIGHEST)
        return placed.reshape(count, quarter, 2 * width).astype(jnp.bfloat16)

    def project_modes(coupling):
        near = jnp.einsum(
            "sqi,smi->sqm", coupling[:, :, :width], left_modes, preferred_element_type=jnp.float32
        )
        far = jnp.einsum(
            "sqi,smi->sqm", coupling[:, :, width:], right_modes, preferred_element_type=jnp.float32
        )
        return jnp.concatenate([near, far], axis=2).reshape(lax.axis_size("sub"), -1, 2 * modes)

    coupling_k, coupling_m = (couple_one(k_blocks), couple_one(m_blocks))
    reduced_k = project_modes(coupling_k)
    reduced_m = project_modes(coupling_m)
    grid_k, grid_m = (
        lax.all_to_all(reduced_k, "sub", split_axis=0, concat_axis=0, tiled=True),
        lax.all_to_all(reduced_m, "sub", split_axis=0, concat_axis=0, tiled=True),
    )
    return (grid_k[None, None], grid_m[None, None])


def solution(mesh):
    placed = (
        P("sub", "grp", None),
        P("sub", "grp", None),
        P("sub", None, None, None),
        P("sub", None, None, None),
        P("sub", None),
        P("sub", None),
        P("sub"),
    )
    return jax.shard_map(
        per_device,
        mesh=mesh,
        in_specs=placed,
        out_specs=(P("sub", "grp", None, None, None), P("sub", "grp", None, None, None)),
        check_vma=False,
    )
```

profile of v0, /device:TPU:0, one launch (start us, length us, event | category | flops | bytes accessed | tf_op | source)
XLA Modules:
  0.0 405.1 jit_solution(12655818714770346698)
XLA Ops:
  9.1 2.4 fusion.22
  11.6 6.6 %fusion.10 = f32[8,24,100,128]{3,2,1,0:T(8,128)S(1)} fusion(bf16[8,24,128,128]{3,2,1,0:T(8,128)(2,1)} %param.10, bf16[8,24,100,128]{3,1,2,0:T(8,128)(2,1)S(1)} %fusion.22), kind=kOutput, calls=%fused_computation.9 | convolution fusion | flops 629145600 | bytes 21037056 | tf_op jit(solution)/shard_map/snqc,sncd->snqd/dot_general | solution.py:36
  18.2 8.0 %convert_bitcast_fusion = bf16[8,100,32,128]{3,2,1,0:T(8,128)(2,1)} fusion(f32[8,24,100,128]{3,2,1,0:T(8,128)S(1)} %fusion.10, s32[8,24]{1,0:T(8,128)S(1)} %copy-done.7), kind=kOutput, calls=%fused_computation.7 | convolution fusion | flops 947001344 | bytes 16384768 | tf_op jit(solution)/shard_map/snqd,snb->sqbd/dot_general | solution.py:37
  26.3 9.3 %reshape.38 = bf16[8,100,4096]{2,1,0:T(8,128)(2,1)} reshape(bf16[8,100,32,128]{3,2,1,0:T(8,128)(2,1)} %convert_bitcast_fusion) | data formatting | bytes 13107200 | tf_op jit(solution)/shard_map/convert_element_type | solution.py:38
  35.6 11.0 %fusion.12 = f32[8,24,100,128]{3,2,1,0:T(8,128)} fusion(bf16[8,24,128,128]{3,2,1,0:T(8,128)(2,1)} %param.9, bf16[8,24,100,128]{3,1,2,0:T(8,128)(2,1)} %copy-done.2), kind=kOutput, calls=%fused_computation.11 | convolution fusion | flops 629145600 | bytes 21037056 | tf_op jit(solution)/shard_map/snqc,sncd->snqd/dot_general | solution.py:36
  46.6 192.5 %all-gather.2.cloned.1.call-done = bf16[8,400,2048]{2,0,1:T(8,128)(2,1)} async-done(((bf16[8,100,2048]{2,0,1:T(8,128)(2,1)}), bf16[8,400,2048]{2,0,1:T(8,128)(2,1)}) %all-gather.2.cloned.1.call-update) | async-done | bytes 13107216 | tf_op jit(solution)/shard_map/all_gather | solution.py:18
  239.1 13.2 %copy.28 = bf16[8,400,2048]{2,1,0:T(8,128)(2,1)S(1)} copy(bf16[8,400,2048]{2,0,1:T(8,128)(2,1)} %all-gather.2.cloned.1.call-done) | data formatting | bytes 26214400 | tf_op jit(solution)/shard_map/all_gather | solution.py:18
  252.3 4.7 %copy-done.4 = bf16[8,400,2048]{2,1,0:T(8,128)(2,1)} copy-done((bf16[8,400,2048]{2,1,0:T(8,128)(2,1)}, bf16[8,400,2048]{2,1,0:T(8,128)(2,1)S(1)}, u32[]{:S(2)}) %copy-start.4) | copy-done | bytes 13107224
  257.1 3.2 collective-permute-start
  260.3 8.0 %convert_bitcast_fusion.1 = bf16[8,100,32,128]{3,2,1,0:T(8,128)(2,1)} fusion(f32[8,24,100,128]{3,2,1,0:T(8,128)S(1)} %copy-done.3, s32[8,24]{1,0:T(8,128)S(1)} %copy-done.7), kind=kOutput, calls=%fused_computation.8 | convolution fusion | flops 947001344 | bytes 16384768 | tf_op jit(solution)/shard_map/snqd,snb->sqbd/dot_general | solution.py:37
  268.3 9.2 %reshape.37 = bf16[8,100,4096]{2,1,0:T(8,128)(2,1)} reshape(bf16[8,100,32,128]{3,2,1,0:T(8,128)(2,1)} %convert_bitcast_fusion.1) | data formatting | bytes 13107200 | tf_op jit(solution)/shard_map/convert_element_type | solution.py:38
  277.5 10.7 %slice.26 = bf16[7,400,2048]{2,1,0:T(8,128)(2,1)} slice(bf16[8,400,2048]{2,1,0:T(8,128)(2,1)} %copy-done.4), slice={[0:7], [0:400], [0:2048]} | slice | bytes 22937600 | tf_op jit(solution)/shard_map/slice | solution.py:20
  288.2 14.3 %fusion.14 = f32[8,100,400]{1,2,0:T(8,128)} fusion(bf16[8,100,4096]{2,1,0:T(8,128)(2,1)} %reshape.38, bf16[8,400,2048]{2,0,1:T(8,128)(2,1)} %all-gather.2.cloned.1.call-done), kind=kOutput, calls=%fused_computation.13 | convolution fusion | flops 1310720000 | bytes 17795072 | tf_op jit(solution)/shard_map/sqi,smi->sqm/dot_general | solution.py:44
  302.5 7.9 %fusion.4 = f32[8,100,400]{1,2,0:T(8,128)S(1)} fusion(bf16[7,400,2048]{2,1,0:T(8,128)(2,1)} %slice.26, bf16[1,400,2048]{2,1,0:T(8,128)(2,1)} %bitcast.7, bf16[8,100,4096]{2,1,0:T(8,128)(2,1)} %reshape.38), kind=kOutput, calls=%fused_computation.5 | convolution fusion | flops 1317273600 | bytes 17795072 | tf_op jit(solution)/shard_map/sqi,smi->sqm/dot_general | solution.py:41
  310.6 2.6 copy.39
  313.2 4.4 %all-to-all-start.1 = ((f32[8,100,800]{2,1,0:T(8,128)}), f32[8,100,800]{2,1,0:T(8,128)}, u32[]{:S(2)}, u32[]{:S(2)}) async-start(f32[8,100,800]{2,1,0:T(8,128)} %copy.39), calls=%async_computation.1 | async-start | bytes 5963776 | tf_op jit(solution)/shard_map/all_to_all | solution.py:54
  317.6 14.3 %fusion.17 = f32[8,100,400]{1,2,0:T(8,128)} fusion(bf16[8,100,4096]{2,1,0:T(8,128)(2,1)} %reshape.37, bf16[8,400,2048]{2,0,1:T(8,128)(2,1)} %all-gather.2.cloned.1.call-done), kind=kOutput, calls=%fused_computation.16 | convolution fusion | flops 1310720000 | bytes 17795072 | tf_op jit(solution)/shard_map/sqi,smi->sqm/dot_general | solution.py:44
  331.9 7.7 %fusion.5 = f32[8,100,400]{1,2,0:T(8,128)S(1)} fusion(bf16[7,400,2048]{2,1,0:T(8,128)(2,1)} %slice.26, bf16[1,400,2048]{2,1,0:T(8,128)(2,1)} %bitcast.7, bf16[8,100,4096]{2,1,0:T(8,128)(2,1)} %reshape.37), kind=kOutput, calls=%fused_computation.6 | convolution fusion | flops 1317273600 | bytes 17795072 | tf_op jit(solution)/shard_map/sqi,smi->sqm/dot_general | solution.py:41
  339.8 2.5 copy.32
  342.3 11.4 %all-to-all-done.1 = f32[8,100,800]{2,1,0:T(8,128)} async-done(((f32[8,100,800]{2,1,0:T(8,128)}), f32[8,100,800]{2,1,0:T(8,128)}, u32[]{:S(2)}, u32[]{:S(2)}) %all-to-all-start.1) | async-done | bytes 2560032 | tf_op jit(solution)/shard_map/all_to_all | solution.py:54
  353.8 4.4 %all-to-all-start = ((f32[8,100,800]{2,1,0:T(8,128)}), f32[8,100,800]{2,1,0:T(8,128)}, u32[]{:S(2)}, u32[]{:S(2)}) async-start(f32[8,100,800]{2,1,0:T(8,128)} %copy.32), calls=%async_computation | async-start | bytes 5963776 | tf_op jit(solution)/shard_map/all_to_all | solution.py:53
  358.2 4.1 %copy.41 = f32[1,1,8,100,800]{4,2,3,1,0:T(8,128)} copy(f32[1,1,8,100,800]{4,3,2,1,0:T(8,128)} %bitcast.11) | data formatting | bytes 5120000
  362.3 32.0 %all-to-all-done = f32[8,100,800]{2,1,0:T(8,128)} async-done(((f32[8,100,800]{2,1,0:T(8,128)}), f32[8,100,800]{2,1,0:T(8,128)}, u32[]{:S(2)}, u32[]{:S(2)}) %all-to-all-start) | async-done | bytes 2560032 | tf_op jit(solution)/shard_map/all_to_all | solution.py:53
  394.3 4.0 copy.40
  (22 shorter events, 2.5 us)
Async XLA Ops:
  7.2 1.9 copy-start
  7.2 231.9 %all-gather.2.cloned.1.call-start = ((), (), s32[]{:S(2)}) async-start(), calls=%async_computation.2 | async-start | bytes 16384000 | tf_op jit(solution)/shard_map/all_gather | solution.py:18
  11.5 6.7 %copy-start.2 = (bf16[8,24,100,128]{3,1,2,0:T(8,128)(2,1)}, bf16[8,24,100,128]{3,1,2,0:T(8,128)(2,1)S(1)}, u32[]{:S(2)}) copy-start(bf16[8,24,100,128]{3,1,2,0:T(8,128)(2,1)S(1)} %fusion.22) | copy-start | bytes 14745604
  11.6 6.7 %copy-start.7 = (s32[8,24]{1,0:T(8,128)S(1)}, s32[8,24]{1,0:T(8,128)}, u32[]{:S(2)}) copy-start(s32[8,24]{1,0:T(8,128)} %param.12) | copy-start | bytes 2308
  239.1 21.2 %copy-start.3 = (f32[8,24,100,128]{3,2,1,0:T(8,128)S(1)}, f32[8,24,100,128]{3,2,1,0:T(8,128)}, u32[]{:S(2)}) copy-start(f32[8,24,100,128]{3,2,1,0:T(8,128)} %fusion.12) | copy-start | bytes 29491204
  252.3 4.7 %copy-start.4 = (bf16[8,400,2048]{2,1,0:T(8,128)(2,1)}, bf16[8,400,2048]{2,1,0:T(8,128)(2,1)S(1)}, u32[]{:S(2)}) copy-start(bf16[8,400,2048]{2,1,0:T(8,128)(2,1)S(1)} %copy.28) | copy-start | bytes 39321604
  257.1 45.4 %collective-permute-start = (bf16[400,2048]{1,0:T(8,128)(2,1)S(1)}, bf16[400,2048]{1,0:T(8,128)(2,1)}, u32[]{:S(2)}, u32[]{:S(2)}) collective-permute-start(bf16[400,2048]{1,0:T(8,128)(2,1)S(1)} %slice_bitcast_fusion), channel_id=1, source_target_pairs={{0,4},{4,8},{8,12},{12,16},{16,20},{20,24},{24,28},{1,5},{5,9},{9,... | collective-permute-start | bytes 4915208 | tf_op jit(solution)/shard_map/ppermute | solution.py:10
  302.5 7.9 %copy-start.5 = (f32[8,100,400]{1,2,0:T(8,128)S(1)}, f32[8,100,400]{1,2,0:T(8,128)}, u32[]{:S(2)}) copy-start(f32[8,100,400]{1,2,0:T(8,128)} %fusion.14) | copy-start | bytes 3840004
  313.2 40.6 %all-to-all-start.1 = ((f32[8,100,800]{2,1,0:T(8,128)}), f32[8,100,800]{2,1,0:T(8,128)}, u32[]{:S(2)}, u32[]{:S(2)}) async-start(f32[8,100,800]{2,1,0:T(8,128)} %copy.39), calls=%async_computation.1 | async-start | bytes 5963776 | tf_op jit(solution)/shard_map/all_to_all | solution.py:54
  331.9 7.7 %copy-start.6 = (f32[8,100,400]{1,2,0:T(8,128)S(1)}, f32[8,100,400]{1,2,0:T(8,128)}, u32[]{:S(2)}) copy-start(f32[8,100,400]{1,2,0:T(8,128)} %fusion.17) | copy-start | bytes 3840004
  353.8 40.6 %all-to-all-start = ((f32[8,100,800]{2,1,0:T(8,128)}), f32[8,100,800]{2,1,0:T(8,128)}, u32[]{:S(2)}, u32[]{:S(2)}) async-start(f32[8,100,800]{2,1,0:T(8,128)} %copy.32), calls=%async_computation | async-start | bytes 5963776 | tf_op jit(solution)/shard_map/all_to_all | solution.py:53
  358.2 40.1 %copy-start.1 = (bf16[8,100,2048]{2,0,1:T(8,128)(2,1)S(1)}, bf16[8,100,2048]{2,0,1:T(8,128)(2,1)}, u32[]{:S(2)}) copy-start(bf16[8,100,2048]{2,0,1:T(8,128)(2,1)} %param.7) | copy-start | bytes 9830404
Sparse Core Ops, SparseCore 0:
  9.6 229.4 all-gather.1
where the time goes:
time: 406 us; the launch traced here: 405 us
  waiting for transfers between devices  237 us (58%)
  matrix products  80.3 us (20%)
  local copies, waits for them, and re-layouts  60.7 us (15%)
  between operations  14.2 us (3%)
  starting transfers between devices  12.1 us (3%)
    all_gather x1, waiting for transfers between devices, per_device(): right_modes = lax.all_gather(psi, 'grp', axis=1, tiled=True)  192 us
    all_to_all x1, waiting for transfers between devices, per_device(): lax.all_to_all(reduced_k, 'sub', split_axis=0, concat_axis=0, tiled=True)  32 us
    dot_general x2, matrix products, project_modes(): jnp.einsum('sqi,smi->sqm', coupling[:, :, width:], right_modes, preferred...  28.6 us
    convert_element_type x2, local copies, waits for them, and re-layouts, couple_one(): return placed.reshape(count, quarter, 2 * width).astype(jnp.bfloat16)  18.6 us
    dot_general x2, matrix products, couple_one(): jnp.einsum('snqc,sncd->snqd', picked, blocks, preferred_element_type=jnp....  17.7 us
    dot_general x2, matrix products, couple_one(): jnp.einsum('snqd,snb->sqbd', term, col_hot, precision=lax.Precision.HIGHEST)  16.1 us
    dot_general x2, matrix products, project_modes(): jnp.einsum('sqi,smi->sqm', coupling[:, :, :width], left_modes, preferred_...  15.6 us
    all_gather x1, local copies, waits for them, and re-layouts, per_device(): right_modes = lax.all_gather(psi, 'grp', axis=1, tiled=True)  13.2 us
  transfers between devices with their start and end apart: 4, of which 3 were waited for; matrix products, arithmetic and copies ran while one was open for 27% of the time, Pallas kernels for 0%

commit v1 on v0

v1 whole, which is shorter than its diff:
```python
import functools

import jax
import jax.numpy as jnp
from jax import lax
from jax.experimental import pallas as pl
from jax.experimental.pallas import tpu as pltpu
from jax.sharding import PartitionSpec as P

EDGE = 128
ROWS = 112
SLOTS = 4
BITE = 4
ROOM = 88
MORE = 16
MIB = 1 << 20
LIGHT = pl.CostEstimate(flops=1, bytes_accessed=1, transcendentals=0)


def up_to(limit, body, unroll=1):
    lax.fori_loop(0, limit, lambda n, _: (body(n), 0)[1], 0, unroll=unroll)


def lanes(block, count=1):
    return pl.ds(pl.multiple_of(block * EDGE, EDGE), count * EDGE)


class Meta:
    def __init__(self, count, slots, blocks_per):
        self.count, self.slots, self.blocks_per = count, slots, blocks_per
        self.keys = (count + 1) * blocks_per
        self.order = 0
        self.start = self.keys + ROOM + MORE
        self.size = self.start + count + 2


def list_kernel(at, live, col, meta, flags):
    def clear(n):
        flags[n] = 0

    up_to(at.keys, clear, unroll=16)
    for i in range(at.count):

        def mark(n, i=i):
            flags[col[i, n] + i * at.blocks_per] = 1

        up_to(live[i], mark)

    def place(key, taken):
        meta[at.order + taken] = key
        return taken + flags[key]

    taken = 0
    for side in range(at.count + 1):
        meta[at.start + side] = taken
        taken = lax.fori_loop(
            side * at.blocks_per, (side + 1) * at.blocks_per, place, taken, unroll=at.blocks_per
        )
    meta[at.start + at.count + 1] = taken

    def fill(n):
        meta[at.order + n] = at.blocks_per

    lax.fori_loop(taken, at.start, lambda n, _: (fill(n), 0)[1], 0)


def listed(at, block_col, live):
    return pl.pallas_call(
        functools.partial(list_kernel, at),
        out_shape=jax.ShapeDtypeStruct((at.size,), jnp.int32),
        in_specs=[pl.BlockSpec(memory_space=pltpu.SMEM)] * 2,
        out_specs=pl.BlockSpec(memory_space=pltpu.SMEM),
        scratch_shapes=[pltpu.SMEM((at.keys,), jnp.int32)],
    )(live, block_col)


def pack_kernel(at, first, room, meta, psi, border, out):
    def one(c):
        key = meta[at.order + first + c]
        side, block = key // at.blocks_per, key % at.blocks_per

        @pl.when(side == 0)
        def _():
            out[:, lanes(c)] = border[:, lanes(block)]

        @pl.when(side > 0)
        def _():
            out[:, lanes(c)] = psi[side - 1, :, lanes(block)]

    up_to(room, one)


def pack(at, first, room, meta, psi, border):
    return pl.pallas_call(
        functools.partial(pack_kernel, at, first, room),
        out_shape=jax.ShapeDtypeStruct((psi.shape[1], room * EDGE), psi.dtype),
        in_specs=[
            pl.BlockSpec(memory_space=pltpu.SMEM),
            pl.BlockSpec(memory_space=pltpu.VMEM),
            pl.BlockSpec(memory_space=pltpu.VMEM),
        ],
        out_specs=pl.BlockSpec(memory_space=pltpu.VMEM),
        compiler_params=pltpu.CompilerParams(vmem_limit_bytes=8 * MIB),
        cost_estimate=LIGHT,
    )(meta, psi, border)


def coupling_kernel(at, room, meta, live, row, col, phi, k_blocks, m_blocks, out, total):
    i = pl.program_id(0)
    modes = phi.shape[1]
    here, middle, end = (meta[at.start + i + n] for n in range(3))
    first = at.blocks_per * i

    def clear(n):
        total[meta[at.order + here + n] - first] = jnp.zeros(total.shape[1:], total.dtype)

    up_to(end - here, clear)

    def add_slots(step):
        terms = []
        for n in range(SLOTS):
            slot = jnp.minimum(step * SLOTS + n, at.slots - 1)
            picked = phi[0, :, lanes(row[i, slot])]
            both = jnp.concatenate([k_blocks[0, slot], m_blocks[0, slot]], axis=1)
            to = jnp.where(step * SLOTS + n < live[i], col[i, slot], 2 * at.blocks_per)
            terms.append((to, jnp.dot(picked, both, preferred_element_type=jnp.float32)))
        for to, term in terms:
            total[to] += term

    up_to((live[i] + SLOTS - 1) // SLOTS, add_slots)

    def put(flavour, c):
        done = total[meta[at.order + c] - first].astype(out.dtype)
        out[flavour * ROWS : flavour * ROWS + modes, lanes(c)] = done[:, :EDGE]
        out[(flavour + 1) * ROWS : (flavour + 1) * ROWS + modes, lanes(c)] = done[:, EDGE:]

    def blank(top, c):
        out[top : top + 2 * ROWS, lanes(c)] = jnp.zeros((2 * ROWS, EDGE), out.dtype)

    up_to(middle - here, lambda n: put(2, here + n))
    up_to(end - middle, lambda n: put(0, middle + n))

    @pl.when(i == 0)
    def _():
        up_to(middle, lambda n: blank(0, n))

    @pl.when(i == at.count - 1)
    def _():
        up_to(room - middle, lambda n: blank(2 * ROWS, middle + n))
        up_to(room - end, lambda n: blank(0, end + n))


def couple(at, room, meta, live, row, col, phi, k_blocks, m_blocks):
    count, modes, width = phi.shape
    slots = k_blocks.shape[1]
    return pl.pallas_call(
        functools.partial(coupling_kernel, at, room),
        out_shape=jax.ShapeDtypeStruct((4 * ROWS, room * EDGE), phi.dtype),
        grid_spec=pltpu.PrefetchScalarGridSpec(
            num_scalar_prefetch=4,
            grid=(count,),
            in_specs=[
                pl.BlockSpec((1, modes, width), lambda i, *_: (i, 0, 0)),
                pl.BlockSpec((1, slots, EDGE, EDGE), lambda i, *_: (i, 0, 0, 0)),
                pl.BlockSpec((1, slots, EDGE, EDGE), lambda i, *_: (i, 0, 0, 0)),
            ],
            out_specs=pl.BlockSpec(
                (4 * ROWS, room * EDGE), lambda i, *_: (0, 0), pipeline_mode=pl.Buffered(1)
            ),
            scratch_shapes=[pltpu.VMEM((2 * at.blocks_per + 1, modes, 2 * EDGE), jnp.float32)],
        ),
        compiler_params=pltpu.CompilerParams(vmem_limit_bytes=56 * MIB),
        cost_estimate=LIGHT,
    )(meta, live, row, col, phi, k_blocks, m_blocks)


def project_kernel(at, cuts, sets, meta, coupling, *refs):
    pieces, many = len(cuts) - 1, sum(sets)
    shards, refs = refs[: many * pieces], refs[many * pieces :]
    out, held, shard, right, total, held_done, shard_done = refs
    modes = shard.shape[1]
    middles = [(low + high) // 2 for low, high in zip(cuts, cuts[1:])]
    bounds = sorted((*cuts, *middles))
    parts = list(zip(bounds, bounds[1:]))
    coming = []
    for n, (low, high) in enumerate(parts):
        to, here = pl.ds(low * EDGE, (high - low) * EDGE), []
        if n % 2 == 0:
            piece = n // 2
            whole = pl.ds(cuts[piece] * EDGE, (cuts[piece + 1] - cuts[piece]) * EDGE)
            for k in range(many):
                one = k * pieces + piece
                here.append(
                    pltpu.make_async_copy(shards[one], shard.at[k, :, whole], shard_done.at[one])
                )
        here.append(pltpu.make_async_copy(coupling.at[:, to], held.at[:, to], held_done.at[n]))
        for copy in here:
            copy.start()
        coming.append(here)
    groups, taken = [], 0
    for size in sets:
        groups.append(range(taken, taken + size))
        taken += size
    right[...] = jnp.zeros(right.shape, right.dtype)
    total[...] = jnp.zeros(total.shape, total.dtype)
    for (low, high), here in zip(parts, coming):
        for copy in here:
            copy.wait()

        def on_side(side, low=low, high=high):
            begin = jnp.maximum(meta[at.start + side], low)
            end = jnp.minimum(meta[at.start + side + 1], high)

            def bite(n):
                want = begin + n * BITE
                first = jnp.minimum(want, high - BITE)
                lane = lax.broadcasted_iota(jnp.int32, (modes, BITE * EDGE), 1) + first * EDGE
                inside = (lane >= want * EDGE) & (lane < end * EDGE)
                for g, group in enumerate(groups):
                    part = shard[group[0], :, lanes(first, BITE)]
                    for other in group[1:]:
                        part = part + shard[other, :, lanes(first, BITE)]
                    part = jnp.where(inside, part, jnp.zeros_like(part))
                    right[g * EDGE : g * EDGE + modes, :] = part
                total[side] += lax.dot_general(
                    held[:, lanes(first, BITE)],
                    right[...],
                    (((1,), (1,)), ((), ())),
                    preferred_element_type=jnp.float32,
                )

            up_to(jnp.maximum(end - begin + BITE - 1, 0) // BITE, bite)

        up_to(at.count + 1, on_side)
    for side in range(at.count + 1):
        for g in range(len(groups)):
            for flavour, (sub, part) in enumerate(
                ((side - 1, 1), (side - 1, 3), (side, 0), (side, 2))
            ):
                if 0 <= sub < at.count:
                    top, to = flavour * ROWS, (g * 4 + part) * modes
                    one = total[side, top : top + modes, g * EDGE : g * EDGE + modes]
                    out[sub, :, to : to + modes] = one.astype(out.dtype)


def project(at, cuts, meta, coupling, groups):
    modes = groups[0][0][0].shape[0]
    flat = [piece for group in groups for shard in group for piece in shard]
    sets = tuple(len(group) for group in groups)
    n = len(groups)
    wide = -(-n * 4 * modes // EDGE) * EDGE
    return pl.pallas_call(
        functools.partial(project_kernel, at, cuts, sets),
        out_shape=jax.ShapeDtypeStruct((at.count, modes, wide), coupling.dtype),
        in_specs=[pl.BlockSpec(memory_space=pltpu.SMEM)]
        + [pl.BlockSpec(memory_space=pltpu.HBM)] * (1 + len(flat)),
        out_specs=pl.BlockSpec(memory_space=pltpu.VMEM),
        scratch_shapes=[
            pltpu.VMEM(coupling.shape, coupling.dtype),
            pltpu.VMEM((sum(sets), modes, coupling.shape[1]), coupling.dtype),
            pltpu.VMEM((n * EDGE, BITE * EDGE), coupling.dtype),
            pltpu.VMEM((at.count + 1, 4 * ROWS, n * EDGE), jnp.float32),
            pltpu.SemaphoreType.DMA((2 * (len(cuts) - 1),)),
            pltpu.SemaphoreType.DMA((len(flat),)),
        ],
        compiler_params=pltpu.CompilerParams(vmem_limit_bytes=56 * MIB),
        cost_estimate=LIGHT,
    )(meta, coupling, *flat)


def assemble_kernel(modes, place, near, late, *refs):
    befores, (grid_k, grid_m, wide) = refs[:-3], refs[-3:]
    own, left, right = ((near, g) for g in range(3))
    second, third = ((late, g) for g in range(2))
    plans = (
        (own, right, second, third),
        (left, own, right, second),
        (second, left, own, right),
        (third, second, left, own),
    )
    for which, grid in enumerate((grid_k, grid_m)):
        for z, plan in enumerate(plans):

            @pl.when(place[0] == z)
            def _(plan=plan, which=which):
                for far in range(2):
                    for h, (part, g) in enumerate(plan):
                        take = (g * 4 + 2 * which + far) * modes
                        at = (4 * far + h) * modes
                        wide[:, :, at : at + modes] = part[:, :, take : take + modes].astype(
                            jnp.float32
                        )

        new = jnp.transpose(wide[...], (1, 0, 2))
        grid[...] = new + befores[which][...] if befores else new


def assemble(place, parts, modes, before=None):
    owners, rows, _ = parts[0].shape
    out = jax.ShapeDtypeStruct((rows, owners, 8 * modes), jnp.float32)
    group = min(owners, 8)
    block = pl.BlockSpec((rows, group, 8 * modes), lambda d, place: (0, d, 0))
    befores = [] if before is None else list(before)
    return pl.pallas_call(
        functools.partial(assemble_kernel, modes),
        out_shape=[out, out],
        grid_spec=pltpu.PrefetchScalarGridSpec(
            num_scalar_prefetch=1,
            grid=(owners // group,),
            in_specs=[
                pl.BlockSpec((group, *part.shape[1:]), lambda d, place: (d, 0, 0)) for part in parts
            ]
            + [block] * len(befores),
            out_specs=[block] * 2,
            scratch_shapes=[pltpu.VMEM((group, rows, 8 * modes), jnp.float32)],
        ),
        input_output_aliases={1 + len(parts) + n: n for n in range(len(befores))},
        compiler_params=pltpu.CompilerParams(vmem_limit_bytes=56 * MIB),
        cost_estimate=LIGHT,
    )(place, *parts, *befores)


def moved(shard, axis, by):
    length = lax.axis_size(axis)
    pairs = [(i, i + by) for i in range(length) if 0 <= i + by < length]
    return lax.ppermute(shard, axis, pairs)


def to_owners(part):
    count, modes, cols = part.shape
    owners = lax.axis_size("sub")
    part = part.reshape(owners, count * modes // owners, cols)
    return lax.all_to_all(part, "sub", split_axis=0, concat_axis=0, tiled=True)


def one_round(at, room, meta, ints, phi, psi, border, k_blocks, m_blocks, beside, before=None):
    modes = phi.shape[1]
    cuts = (0, room // 2, room)
    hold = lax.optimization_barrier

    def both_ways(left, right):
        return moved(left, "grp", 1), moved(right, "grp", -1)

    own_a = pack(at, cuts[0], cuts[1] - cuts[0], meta, psi, border)
    one_a = both_ways(own_a, own_a)
    meta, own_a = hold((meta, own_a))
    own_b = pack(at, cuts[1], cuts[2] - cuts[1], meta, psi, border)
    one_b = both_ways(own_b, own_b)
    one_a, beside, phi = hold((one_a, beside, phi))
    two_a = both_ways(*one_a)
    coupling = couple(at, room, meta, *ints, phi, k_blocks, m_blocks)
    one_b, coupling = hold((one_b, coupling))
    two_b = both_ways(*one_b)
    near = [((own_a, own_b),), ((one_a[0], one_b[0]),), ((one_a[1], one_b[1]),)]
    near = project(at, cuts, meta, coupling, near)
    two_a, near = hold((two_a, near))
    three_a = both_ways(*two_a)
    near = to_owners(near)
    three_a, two_b = hold((three_a, two_b))
    three_b = both_ways(*two_b)
    three_b, near = hold((three_b, near))
    late = [tuple(zip(a, b)) for a, b in ((two_a, two_b), (three_a, three_b))]
    late = to_owners(project(at, cuts, meta, coupling, late))
    place = lax.axis_index("grp").astype(jnp.int32)[None]
    return assemble(place, (near, late), modes, before), beside


def shifted(at, meta, by, room):
    kept = jnp.concatenate([meta[: at.start], jnp.full((at.start,), at.blocks_per, jnp.int32)])
    order = lax.dynamic_slice_in_dim(kept, by, at.start, 0)
    return jnp.concatenate([order, jnp.clip(meta[at.start :] - by, 0, room)])


def per_device(phi, psi, k_blocks, m_blocks, block_row, block_col, live):
    count, modes, width = phi.shape
    at = Meta(count, k_blocks.shape[1], width // EDGE)
    border = moved(psi[count - 1], "sub", 1)
    whole = listed(at, block_col, live)
    ints = (live, block_row, block_col)
    most = lax.pmax(whole[at.start + count + 1], "sub")
    meta = jnp.concatenate([whole[: at.start], jnp.minimum(whole[at.start :], ROOM)])
    grids, most = one_round(at, ROOM, meta, ints, phi, psi, border, k_blocks, m_blocks, most)

    def turned(whole):
        return whole.transpose(1, 0, 2)

    def go_on(state):
        return state[0] < most

    def further(state):
        done, phi, psi, before = state[0], state[1], state[2], state[3:]
        phi, psi = (turned(one) for one in lax.optimization_barrier((phi, psi)))
        meta = shifted(at, whole, done, MORE)
        after, _ = one_round(
            at, MORE, meta, ints, phi, psi, border, k_blocks, m_blocks, done, before
        )
        return (done + MORE, *state[1:3], *after)

    state = lax.while_loop(go_on, further, (jnp.int32(ROOM), turned(phi), turned(psi), *grids))
    return tuple(turned(grid)[None, None] for grid in state[3:])


def solution(mesh):
    placed = (
        P("sub", "grp", None),
        P("sub", "grp", None),
        P("sub", None, None, None),
        P("sub", None, None, None),
        P("sub", None),
        P("sub", None),
        P("sub"),
    )
    return jax.shard_map(
        per_device,
        mesh=mesh,
        in_specs=placed,
        out_specs=(P("sub", "grp", None, None, None), P("sub", "grp", None, None, None)),
        check_vma=False,
    )
```

time: 406 us -> 231 us (0.57)
  waiting for transfers between devices: 237 us -> 80.8 us
  matrix products: 80.3 us -> 0 us
  Pallas kernels: 0 us -> 60.4 us
  starting transfers between devices: 12.1 us -> 58.6 us
  local copies, waits for them, and re-layouts: 60.7 us -> 15.2 us
  blocking collectives: 0 us -> 13.2 us
  between operations: 14.2 us -> 1.04 us
    all_gather x1 -> x0, waiting for transfers between devices: 192 us -> none  [per_device(): right_modes = lax.all_gather(psi, 'grp', axis=1, tiled=True)]
    dot_general x9 -> x0, matrix products: 80.3 us -> none  [the longest x2 28.6 us: project_modes(): jnp.einsum('sqi,smi->sqm', coupling[:, :, width:], right_modes, preferred...]
    ppermute x1 -> x13, waiting for transfers between devices: 0.01 us -> 64 us  [moved(): return lax.ppermute(shard, axis, pairs)]
    pallas_call x0 -> x7, Pallas kernels: none -> 60.4 us  [the longest x2 28.2 us: project(): pl.pallas_call(functools.partial(project_kernel, at, cuts, sets), out_sha...]
    ppermute x1 -> x13, starting transfers between devices: 3.16 us -> 36.3 us  [moved(): return lax.ppermute(shard, axis, pairs)]
    all_to_all x2, waiting for transfers between devices: 43.4 us -> 16.7 us  [to_owners(): return lax.all_to_all(part, 'sub', split_axis=0, concat_axis=0, tiled=True)]
    convert_element_type x2 -> x0, local copies, waits for them, and re-layouts: 18.6 us -> none  [couple_one(): return placed.reshape(count, quarter, 2 * width).astype(jnp.bfloat16)]
    all_to_all x2, starting transfers between devices: 8.87 us -> 22.3 us  [to_owners(): return lax.all_to_all(part, 'sub', split_axis=0, concat_axis=0, tiled=True)]
  transfers between devices with their start and end apart: 4 -> 15, of which waited for: 3 -> 8; matrix products, arithmetic and copies ran while one was open for 27% -> 4% of each run, Pallas kernels for 0% -> 16%
where the time goes in v1:
time: 231 us; the launch traced here: 230 us
  waiting for transfers between devices  80.8 us (35%)
  Pallas kernels  60.4 us (26%)
  starting transfers between devices  58.6 us (25%)
  local copies, waits for them, and re-layouts  15.2 us (7%)
  blocking collectives  13.2 us (6%)
    ppermute x13, waiting for transfers between devices, moved(): return lax.ppermute(shard, axis, pairs)  64 us
    ppermute x13, starting transfers between devices, moved(): return lax.ppermute(shard, axis, pairs)  36.3 us
    pallas_call x2, Pallas kernels, project(): pl.pallas_call(functools.partial(project_kernel, at, cuts, sets), out_sha...  28.2 us
    all_to_all x2, starting transfers between devices, to_owners(): return lax.all_to_all(part, 'sub', split_axis=0, concat_axis=0, tiled=True)  22.3 us
    pallas_call x1, Pallas kernels, couple(): pl.pallas_call(functools.partial(coupling_kernel, at, room), out_shape=ja...  17 us
    all_to_all x2, waiting for transfers between devices, to_owners(): return lax.all_to_all(part, 'sub', split_axis=0, concat_axis=0, tiled=True)  16.7 us
    pmax x1, blocking collectives, per_device(): most = lax.pmax(whole[at.start + count + 1], 'sub')  13.2 us
    unnamed x28, local copies, waits for them, and re-layouts  9.14 us
  transfers between devices with their start and end apart: 15, of which 8 were waited for; matrix products, arithmetic and copies ran while one was open for 4% of the time, Pallas kernels for 16%

profile of v1, /device:TPU:0, one launch (start us, length us, event | category | flops | bytes accessed | tf_op | source)
XLA Modules:
  0.0 230.0 jit_solution(7743682589297115703)
XLA Ops:
  0.7 3.7 %copy.21.psi = bf16[8,100,2048]{2,1,0:T(8,128)(2,1)S(1)} copy(bf16[8,100,2048]{2,0,1:T(8,128)(2,1)} %param.10) | data formatting | bytes 6553600 | tf_op args[1]
  8.7 3.2 %shard_map.86 = s32[258]{0:T(512)S(1)} custom-call(s32[8]{0:T(128)S(1)} %copy-done.26, s32[8,24]{1,0:T(8,128)S(1)} %copy-done.24), custom_call_target="tpu_custom_call" | custom-call | tf_op jit(solution)/shard_map/pallas_call | solution.py:68
  12.1 3.6 %shard_map.87.refs_0_ = bf16[100,5632]{1,0:T(8,128)(2,1)S(1)} custom-call(s32[258]{0:T(512)S(1)} %pad_add_fusion.1.meta, bf16[8,100,2048]{2,1,0:T(8,128)(2,1)} %copy-done.6, bf16[100,2048]{1,0:T(8,128)(2,1)S(1)} %collective-permute-done.12.border), custom_call_target="tpu_custom_call" | custom-call | flops 1 | bytes 1 | tf_op jit(solution)/shard_map/pallas_call | solution.py:94
  15.7 5.4 %collective-permute-start.13 = (bf16[100,5632]{1,0:T(8,128)(2,1)S(1)}, bf16[100,5632]{1,0:T(8,128)(2,1)}, u32[]{:S(2)}, u32[]{:S(2)}) collective-permute-start(bf16[100,5632]{1,0:T(8,128)(2,1)S(1)} %shard_map.87.refs_0_), channel_id=1, source_target_pairs={{0,1},{1,2},{2,3},{4,5},{5,6},{6,7},{8,9},{9,10},{10,11},{12,13},{... | collective-permute-start | bytes 3379208 | tf_op jit(solution)/shard_map/ppermute | solution.py:326
  24.9 5.6 %collective-permute-start.17 = (bf16[100,5632]{1,0:T(8,128)(2,1)S(1)}, bf16[100,5632]{1,0:T(8,128)(2,1)}, u32[]{:S(2)}, u32[]{:S(2)}) collective-permute-start(bf16[100,5632]{1,0:T(8,128)(2,1)S(1)} %shard_map.88.refs_1_), channel_id=1, source_target_pairs={{0,1},{1,2},{2,3},{4,5},{5,6},{6,7},{8,9},{9,10},{10,11},{12,13},{... | collective-permute-start | bytes 3379208 | tf_op jit(solution)/shard_map/ppermute | solution.py:326
  31.8 13.2 %pmax.7 = s32[]{:T(128)} all-reduce(s32[]{:T(128)} %bitcast.5), channel_id=1, replica_groups=mesh['sub'=8,'grp'=4] {'sub'}, use_global_device_ids=true, to_apply=%region_0.0 | all-reduce | flops 1 | bytes 8 | tf_op jit(solution)/shard_map/pmax | solution.py:380
  45.0 4.5 %collective-permute-done.14.refs_4_ = bf16[100,5632]{1,0:T(8,128)(2,1)} collective-permute-done((bf16[100,5632]{1,0:T(8,128)(2,1)S(1)}, bf16[100,5632]{1,0:T(8,128)(2,1)}, u32[]{:S(2)}, u32[]{:S(2)}) %collective-permute-start.14) | collective-permute-done | bytes 1126432 | tf_op jit(solution)/shard_map/ppermute | solution.py:326
  53.3 5.4 %copy.14.phi = bf16[8,100,2048]{2,1,0:T(8,128)(2,1)} copy(bf16[8,100,2048]{2,0,1:T(8,128)(2,1)} %param.9) | data formatting | bytes 6553600 | tf_op jit(solution)/shard_map/optimization_barrier | solution.py:349
  58.8 17.0 %shard_map.89.coupling = bf16[448,11264]{1,0:T(8,128)(2,1)} custom-call(s32[258]{0:T(512)} %copy-done.5, s32[8]{0:T(128)S(1)} %copy-done.26, s32[8,24]{1,0:T(8,128)S(1)} %copy-done.25, s32[8,24]{1,0:T(8,128)S(1)} %copy-done.24, bf16[8,100,2048]{2,1,0:T(8,128)(2,1)} %copy.14.phi, bf16[8,24,128,128]{3,2,1,0:T(8,128)(2,1)} %k_blocks.1, ...), custom_call_target="tpu_custom_call" | custom-call | flops 1 | bytes 1 | tf_op jit(solution)/shard_map/pallas_call | solution.py:156
  75.7 5.6 %collective-permute-start.21 = (bf16[100,5632]{1,0:T(8,128)(2,1)}, bf16[100,5632]{1,0:T(8,128)(2,1)}, u32[]{:S(2)}, u32[]{:S(2)}) collective-permute-start(bf16[100,5632]{1,0:T(8,128)(2,1)} %collective-permute-done.17.refs_3_), channel_id=1, source_target_pairs={{0,1},{1,2},{2,3},{4,5},{5,6},{6,7},{8,9},{9,10},{10,11},{12,13},{... | collective-permute-start | bytes 3379208 | tf_op jit(solution)/shard_map/ppermute | solution.py:326
  82.6 15.1 %shard_map.90 = bf16[8,100,1280]{2,1,0:T(8,128)(2,1)} custom-call(s32[258]{0:T(512)} %copy-done.5, bf16[448,11264]{1,0:T(8,128)(2,1)} %shard_map.89.coupling, bf16[100,5632]{1,0:T(8,128)(2,1)} %copy-done.2, bf16[100,5632]{1,0:T(8,128)(2,1)} %copy-done.3, bf16[100,5632]{1,0:T(8,128)(2,1)} %collective-permute-done.13.refs_2_, ...), custom_call_target="tpu_custom_call" | custom-call | flops 1 | bytes 1 | tf_op jit(solution)/shard_map/pallas_call | solution.py:252
  99.7 3.7 %collective-permute-start.19 = (bf16[100,5632]{1,0:T(8,128)(2,1)S(1)}, bf16[100,5632]{1,0:T(8,128)(2,1)}, u32[]{:S(2)}, u32[]{:S(2)}) collective-permute-start(bf16[100,5632]{1,0:T(8,128)(2,1)S(1)} %collective-permute-done.15.refs_0_), channel_id=1, source_target_pairs={{0,1},{1,2},{2,3},{4,5},{5,6},{6,7},{8,9},{9,10},{10,11},{12,13},{... | collective-permute-start | bytes 3379208 | tf_op jit(solution)/shard_map/ppermute | solution.py:326
  104.7 16.5 %all-to-all-start.2 = ((bf16[8,100,1280]{2,1,0:T(8,128)(2,1)}), bf16[8,100,1280]{2,1,0:T(8,128)(2,1)S(1)}, u32[]{:S(2)}, u32[]{:S(2)}) async-start(bf16[8,100,1280]{2,1,0:T(8,128)(2,1)} %shard_map.90), calls=%async_computation.2 | async-start | bytes 4259840 | tf_op jit(solution)/shard_map/all_to_all | solution.py:333
  121.2 3.7 %collective-permute-done.22.refs_3_ = bf16[100,5632]{1,0:T(8,128)(2,1)} collective-permute-done((bf16[100,5632]{1,0:T(8,128)(2,1)}, bf16[100,5632]{1,0:T(8,128)(2,1)}, u32[]{:S(2)}, u32[]{:S(2)}) %collective-permute-start.22) | collective-permute-done | bytes 1126432 | tf_op jit(solution)/shard_map/ppermute | solution.py:326
  124.8 19.3 %collective-permute-done.19.refs_4_ = bf16[100,5632]{1,0:T(8,128)(2,1)} collective-permute-done((bf16[100,5632]{1,0:T(8,128)(2,1)S(1)}, bf16[100,5632]{1,0:T(8,128)(2,1)}, u32[]{:S(2)}, u32[]{:S(2)}) %collective-permute-start.19) | collective-permute-done | bytes 1126432 | tf_op jit(solution)/shard_map/ppermute | solution.py:326
  144.1 5.8 %collective-permute-done.20.refs_6_ = bf16[100,5632]{1,0:T(8,128)(2,1)} collective-permute-done((bf16[100,5632]{1,0:T(8,128)(2,1)}, bf16[100,5632]{1,0:T(8,128)(2,1)}, u32[]{:S(2)}, u32[]{:S(2)}) %collective-permute-start.20) | collective-permute-done | bytes 1126432 | tf_op jit(solution)/shard_map/ppermute | solution.py:326
  149.9 3.5 %collective-permute-start.23 = (bf16[100,5632]{1,0:T(8,128)(2,1)}, bf16[100,5632]{1,0:T(8,128)(2,1)}, u32[]{:S(2)}, u32[]{:S(2)}) collective-permute-start(bf16[100,5632]{1,0:T(8,128)(2,1)} %collective-permute-done.21.refs_1_), channel_id=1, source_target_pairs={{0,1},{1,2},{2,3},{4,5},{5,6},{6,7},{8,9},{9,10},{10,11},{12,13},{... | collective-permute-start | bytes 3379208 | tf_op jit(solution)/shard_map/ppermute | solution.py:326
  154.7 23.1 %collective-permute-done.23.refs_5_ = bf16[100,5632]{1,0:T(8,128)(2,1)} collective-permute-done((bf16[100,5632]{1,0:T(8,128)(2,1)}, bf16[100,5632]{1,0:T(8,128)(2,1)}, u32[]{:S(2)}, u32[]{:S(2)}) %collective-permute-start.23) | collective-permute-done | bytes 1126432 | tf_op jit(solution)/shard_map/ppermute | solution.py:326
  177.8 5.7 %collective-permute-done.24.refs_7_ = bf16[100,5632]{1,0:T(8,128)(2,1)} collective-permute-done((bf16[100,5632]{1,0:T(8,128)(2,1)}, bf16[100,5632]{1,0:T(8,128)(2,1)}, u32[]{:S(2)}, u32[]{:S(2)}) %collective-permute-start.24) | collective-permute-done | bytes 1126432 | tf_op jit(solution)/shard_map/ppermute | solution.py:326
  183.6 13.1 %shard_map.91 = bf16[8,100,896]{2,1,0:T(8,128)(2,1)} custom-call(s32[258]{0:T(512)} %copy-done.5, bf16[448,11264]{1,0:T(8,128)(2,1)} %shard_map.89.coupling, bf16[100,5632]{1,0:T(8,128)(2,1)} %copy-done.23, bf16[100,5632]{1,0:T(8,128)(2,1)} %collective-permute-done.21.refs_1_, bf16[100,5632]{1,0:T(8,128)(2,1)} %collective-permute-done.16.refs_2_, ...), custom_call_target="tpu_custom_call" | custom-call | flops 1 | bytes 1 | tf_op jit(solution)/shard_map/pallas_call | solution.py:252
  196.7 5.8 %all-to-all-start.3 = ((bf16[8,100,896]{2,1,0:T(8,128)(2,1)}), bf16[8,100,896]{2,1,0:T(8,128)(2,1)}, u32[]{:S(2)}, u32[]{:S(2)}) async-start(bf16[8,100,896]{2,1,0:T(8,128)(2,1)} %shard_map.91), calls=%async_computation.3 | async-start | bytes 2981888 | tf_op jit(solution)/shard_map/all_to_all | solution.py:333
  202.5 3.5 %copy.20 = bf16[8,100,2048]{2,1,0:T(8,128)(2,1)} copy(bf16[8,100,2048]{2,0,1:T(8,128)(2,1)S(1)} %copy-done.12) | data formatting | bytes 6553600 | tf_op args[0]
  206.0 16.7 %all-to-all-done.3.late = bf16[8,100,896]{2,1,0:T(8,128)(2,1)} async-done(((bf16[8,100,896]{2,1,0:T(8,128)(2,1)}), bf16[8,100,896]{2,1,0:T(8,128)(2,1)}, u32[]{:S(2)}, u32[]{:S(2)}) %all-to-all-start.3) | async-done | bytes 1433632 | tf_op jit(solution)/shard_map/all_to_all | solution.py:333
  222.8 6.5 %shard_map.92 = (f32[100,8,800]{2,1,0:T(8,128)}, f32[100,8,800]{2,1,0:T(8,128)}) custom-call(s32[1]{0:T(128)} %bitcast.3.place, bf16[8,100,1280]{2,1,0:T(8,128)(2,1)} %copy-done.13, bf16[8,100,896]{2,1,0:T(8,128)(2,1)} %all-to-all-done.3.late), custom_call_target="tpu_custom_call" | custom-call | flops 1 | bytes 1 | tf_op jit(solution)/shard_map/pallas_call | solution.py:304
  (49 shorter events, 19.8 us)
Async XLA Ops:
  6.3 5.8 %collective-permute-start.12 = (bf16[100,2048]{1,0:T(8,128)(2,1)S(1)}, bf16[100,2048]{1,0:T(8,128)(2,1)S(1)}, u32[]{:S(2)}, u32[]{:S(2)}) collective-permute-start(bf16[100,2048]{1,0:T(8,128)(2,1)S(1)} %slice_bitcast_fusion), channel_id=1, source_target_pairs={{0,4},{4,8},{8,12},{12,16},{16,20},{20,24},{24,28},{1,5},{5,9},{9,... | collective-permute-start | bytes 1228808 | tf_op jit(solution)/shard_map/ppermute | solution.py:326
  12.0 10.9 %copy-start.5 = (s32[258]{0:T(512)}, s32[258]{0:T(512)S(1)}, u32[]{:S(2)}) copy-start(s32[258]{0:T(512)S(1)} %pad_add_fusion.1.meta) | copy-start | bytes 3100
  12.0 10.9 %copy-start.7 = (bf16[8,100,2048]{2,1,0:T(8,128)(2,1)S(1)}, bf16[8,100,2048]{2,1,0:T(8,128)(2,1)}, u32[]{:S(2)}) copy-start(bf16[8,100,2048]{2,1,0:T(8,128)(2,1)} %copy-done.6) | copy-start | bytes 9830404
  12.0 10.8 %copy-start.10 = (bf16[100,2048]{1,0:T(8,128)(2,1)}, bf16[100,2048]{1,0:T(8,128)(2,1)S(1)}, u32[]{:S(2)}) copy-start(bf16[100,2048]{1,0:T(8,128)(2,1)S(1)} %collective-permute-done.12.border) | copy-start | bytes 1228804
  15.7 29.3 %collective-permute-start.13 = (bf16[100,5632]{1,0:T(8,128)(2,1)S(1)}, bf16[100,5632]{1,0:T(8,128)(2,1)}, u32[]{:S(2)}, u32[]{:S(2)}) collective-permute-start(bf16[100,5632]{1,0:T(8,128)(2,1)S(1)} %shard_map.87.refs_0_), channel_id=1, source_target_pairs={{0,1},{1,2},{2,3},{4,5},{5,6},{6,7},{8,9},{9,10},{10,11},{12,13},{... | collective-permute-start | bytes 3379208 | tf_op jit(solution)/shard_map/ppermute | solution.py:326
  21.0 28.5 %collective-permute-start.14 = (bf16[100,5632]{1,0:T(8,128)(2,1)S(1)}, bf16[100,5632]{1,0:T(8,128)(2,1)}, u32[]{:S(2)}, u32[]{:S(2)}) collective-permute-start(bf16[100,5632]{1,0:T(8,128)(2,1)S(1)} %shard_map.87.refs_0_), channel_id=1, source_target_pairs={{1,0},{2,1},{3,2},{5,4},{6,5},{7,6},{9,8},{10,9},{11,10},{13,12},{... | collective-permute-start | bytes 3379208 | tf_op jit(solution)/shard_map/ppermute | solution.py:326
  24.9 33.9 %copy-start.3 = (bf16[100,5632]{1,0:T(8,128)(2,1)}, bf16[100,5632]{1,0:T(8,128)(2,1)S(1)}, u32[]{:S(2)}) copy-start(bf16[100,5632]{1,0:T(8,128)(2,1)S(1)} %shard_map.88.refs_1_) | copy-start | bytes 3379204
  24.9 50.8 %collective-permute-start.17 = (bf16[100,5632]{1,0:T(8,128)(2,1)S(1)}, bf16[100,5632]{1,0:T(8,128)(2,1)}, u32[]{:S(2)}, u32[]{:S(2)}) collective-permute-start(bf16[100,5632]{1,0:T(8,128)(2,1)S(1)} %shard_map.88.refs_1_), channel_id=1, source_target_pairs={{0,1},{1,2},{2,3},{4,5},{5,6},{6,7},{8,9},{9,10},{10,11},{12,13},{... | collective-permute-start | bytes 3379208 | tf_op jit(solution)/shard_map/ppermute | solution.py:326
  30.5 45.2 %collective-permute-start.18 = (bf16[100,5632]{1,0:T(8,128)(2,1)S(1)}, bf16[100,5632]{1,0:T(8,128)(2,1)}, u32[]{:S(2)}, u32[]{:S(2)}) collective-permute-start(bf16[100,5632]{1,0:T(8,128)(2,1)S(1)} %shard_map.88.refs_1_), channel_id=1, source_target_pairs={{1,0},{2,1},{3,2},{5,4},{6,5},{7,6},{9,8},{10,9},{11,10},{13,12},{... | collective-permute-start | bytes 3379208 | tf_op jit(solution)/shard_map/ppermute | solution.py:326
  45.0 13.8 %copy-start.25 = (s32[8,24]{1,0:T(8,128)S(1)}, s32[8,24]{1,0:T(8,128)}, u32[]{:S(2)}) copy-start(s32[8,24]{1,0:T(8,128)} %row.1) | copy-start | bytes 2308
  49.5 48.3 %collective-permute-start.15 = (bf16[100,5632]{1,0:T(8,128)(2,1)}, bf16[100,5632]{1,0:T(8,128)(2,1)S(1)}, u32[]{:S(2)}, u32[]{:S(2)}) collective-permute-start(bf16[100,5632]{1,0:T(8,128)(2,1)} %collective-permute-done.13.refs_2_), channel_id=1, source_target_pairs={{0,1},{1,2},{2,3},{4,5},{5,6},{6,7},{8,9},{9,10},{10,11},{12,13},{... | collective-permute-start | bytes 3379208 | tf_op jit(solution)/shard_map/ppermute | solution.py:326
  52.0 47.7 %collective-permute-start.16 = (bf16[100,5632]{1,0:T(8,128)(2,1)}, bf16[100,5632]{1,0:T(8,128)(2,1)}, u32[]{:S(2)}, u32[]{:S(2)}) collective-permute-start(bf16[100,5632]{1,0:T(8,128)(2,1)} %collective-permute-done.14.refs_4_), channel_id=1, source_target_pairs={{1,0},{2,1},{3,2},{5,4},{6,5},{7,6},{9,8},{10,9},{11,10},{13,12},{... | collective-permute-start | bytes 3379208 | tf_op jit(solution)/shard_map/ppermute | solution.py:326
  75.7 45.4 %collective-permute-start.21 = (bf16[100,5632]{1,0:T(8,128)(2,1)}, bf16[100,5632]{1,0:T(8,128)(2,1)}, u32[]{:S(2)}, u32[]{:S(2)}) collective-permute-start(bf16[100,5632]{1,0:T(8,128)(2,1)} %collective-permute-done.17.refs_3_), channel_id=1, source_target_pairs={{0,1},{1,2},{2,3},{4,5},{5,6},{6,7},{8,9},{9,10},{10,11},{12,13},{... | collective-permute-start | bytes 3379208 | tf_op jit(solution)/shard_map/ppermute | solution.py:326
  81.3 43.5 %collective-permute-start.22 = (bf16[100,5632]{1,0:T(8,128)(2,1)}, bf16[100,5632]{1,0:T(8,128)(2,1)}, u32[]{:S(2)}, u32[]{:S(2)}) collective-permute-start(bf16[100,5632]{1,0:T(8,128)(2,1)} %collective-permute-done.18.refs_5_), channel_id=1, source_target_pairs={{1,0},{2,1},{3,2},{5,4},{6,5},{7,6},{9,8},{10,9},{11,10},{13,12},{... | collective-permute-start | bytes 3379208 | tf_op jit(solution)/shard_map/ppermute | solution.py:326
  97.8 80.0 %copy-start.23 = (bf16[100,5632]{1,0:T(8,128)(2,1)}, bf16[100,5632]{1,0:T(8,128)(2,1)S(1)}, u32[]{:S(2)}) copy-start(bf16[100,5632]{1,0:T(8,128)(2,1)S(1)} %collective-permute-done.15.refs_0_) | copy-start | bytes 3379204
  99.7 44.4 %collective-permute-start.19 = (bf16[100,5632]{1,0:T(8,128)(2,1)S(1)}, bf16[100,5632]{1,0:T(8,128)(2,1)}, u32[]{:S(2)}, u32[]{:S(2)}) collective-permute-start(bf16[100,5632]{1,0:T(8,128)(2,1)S(1)} %collective-permute-done.15.refs_0_), channel_id=1, source_target_pairs={{0,1},{1,2},{2,3},{4,5},{5,6},{6,7},{8,9},{9,10},{10,11},{12,13},{... | collective-permute-start | bytes 3379208 | tf_op jit(solution)/shard_map/ppermute | solution.py:326
  103.4 46.5 %collective-permute-start.20 = (bf16[100,5632]{1,0:T(8,128)(2,1)}, bf16[100,5632]{1,0:T(8,128)(2,1)}, u32[]{:S(2)}, u32[]{:S(2)}) collective-permute-start(bf16[100,5632]{1,0:T(8,128)(2,1)} %collective-permute-done.16.refs_2_), channel_id=1, source_target_pairs={{1,0},{2,1},{3,2},{5,4},{6,5},{7,6},{9,8},{10,9},{11,10},{13,12},{... | collective-permute-start | bytes 3379208 | tf_op jit(solution)/shard_map/ppermute | solution.py:326
  104.7 50.0 %all-to-all-start.2 = ((bf16[8,100,1280]{2,1,0:T(8,128)(2,1)}), bf16[8,100,1280]{2,1,0:T(8,128)(2,1)S(1)}, u32[]{:S(2)}, u32[]{:S(2)}) async-start(bf16[8,100,1280]{2,1,0:T(8,128)(2,1)} %shard_map.90), calls=%async_computation.2 | async-start | bytes 4259840 | tf_op jit(solution)/shard_map/all_to_all | solution.py:333
  149.9 27.9 %collective-permute-start.23 = (bf16[100,5632]{1,0:T(8,128)(2,1)}, bf16[100,5632]{1,0:T(8,128)(2,1)}, u32[]{:S(2)}, u32[]{:S(2)}) collective-permute-start(bf16[100,5632]{1,0:T(8,128)(2,1)} %collective-permute-done.21.refs_1_), channel_id=1, source_target_pairs={{0,1},{1,2},{2,3},{4,5},{5,6},{6,7},{8,9},{9,10},{10,11},{12,13},{... | collective-permute-start | bytes 3379208 | tf_op jit(solution)/shard_map/ppermute | solution.py:326
  153.4 30.2 %collective-permute-start.24 = (bf16[100,5632]{1,0:T(8,128)(2,1)}, bf16[100,5632]{1,0:T(8,128)(2,1)}, u32[]{:S(2)}, u32[]{:S(2)}) collective-permute-start(bf16[100,5632]{1,0:T(8,128)(2,1)} %collective-permute-done.22.refs_3_), channel_id=1, source_target_pairs={{1,0},{2,1},{3,2},{5,4},{6,5},{7,6},{9,8},{10,9},{11,10},{13,12},{... | collective-permute-start | bytes 3379208 | tf_op jit(solution)/shard_map/ppermute | solution.py:326
  154.7 23.1 %copy-start.13 = (bf16[8,100,1280]{2,1,0:T(8,128)(2,1)}, bf16[8,100,1280]{2,1,0:T(8,128)(2,1)S(1)}, u32[]{:S(2)}) copy-start(bf16[8,100,1280]{2,1,0:T(8,128)(2,1)S(1)} %all-to-all-done.2.near) | copy-start | bytes 6144004
  183.6 19.0 %copy-start.12 = (bf16[8,100,2048]{2,0,1:T(8,128)(2,1)S(1)}, bf16[8,100,2048]{2,0,1:T(8,128)(2,1)}, u32[]{:S(2)}) copy-start(bf16[8,100,2048]{2,0,1:T(8,128)(2,1)} %param.9) | copy-start | bytes 9830404
  196.7 26.1 %all-to-all-start.3 = ((bf16[8,100,896]{2,1,0:T(8,128)(2,1)}), bf16[8,100,896]{2,1,0:T(8,128)(2,1)}, u32[]{:S(2)}, u32[]{:S(2)}) async-start(bf16[8,100,896]{2,1,0:T(8,128)(2,1)} %shard_map.91), calls=%async_computation.3 | async-start | bytes 2981888 | tf_op jit(solution)/shard_map/all_to_all | solution.py:333
  206.0 23.2 %copy-start.8 = (bf16[8,100,2048]{2,1,0:T(8,128)(2,1)S(1)}, bf16[8,100,2048]{2,1,0:T(8,128)(2,1)}, u32[]{:S(2)}) copy-start(bf16[8,100,2048]{2,1,0:T(8,128)(2,1)} %copy-done.6) | copy-start | bytes 9830404
  (4 other events, 27.1 us)

commit v2 on v1

v2 whole, which is shorter than its diff:
```python
import functools

import jax
import jax.numpy as jnp
from jax import lax
from jax.experimental import pallas as pl
from jax.experimental.pallas import tpu as pltpu
from jax.sharding import PartitionSpec as P

EDGE = 128
ROWS = 112
SLOTS = 4
BITE = 4
ROOM = 88
PHI_ROOM = 88
MORE = 16
TALL = 32
MIB = 1 << 20
LIGHT = pl.CostEstimate(flops=1, bytes_accessed=1, transcendentals=0)
HEAVY = pl.CostEstimate(flops=25_000_000_000, bytes_accessed=1, transcendentals=0)


def up_to(limit, body, unroll=1):
    lax.fori_loop(0, limit, lambda n, _: (body(n), 0)[1], 0, unroll=unroll)


def lanes(block, count=1):
    return pl.ds(pl.multiple_of(block * EDGE, EDGE), count * EDGE)


class Meta:
    def __init__(self, count, slots, blocks_per):
        self.count, self.slots, self.blocks_per = count, slots, blocks_per
        self.keys = (count + 1) * blocks_per
        self.order = 0
        self.start = self.keys + max(ROOM + MORE, 2 * PHI_ROOM)
        self.size = self.start + count + 2


def list_kernel(at, shift, live, block, meta, *refs):
    (*places, flags) = refs

    def clear(n):
        flags[n] = 0

    up_to(at.keys, clear, unroll=16)
    for i in range(at.count):

        def mark(n, i=i):
            flags[block[i, n] + (i + shift) * at.blocks_per] = 1

        up_to(live[i], mark)

    def place(key, taken):
        needed = flags[key]
        meta[at.order + taken] = key
        flags[key] = taken
        return taken + needed

    taken = 0
    for side in range(at.count + 1):
        meta[at.start + side] = taken
        taken = lax.fori_loop(
            side * at.blocks_per, (side + 1) * at.blocks_per, place, taken, unroll=at.blocks_per
        )
    meta[at.start + at.count + 1] = taken

    for found in places:
        for i in range(at.count):

            def find(n, i=i, found=found):
                found[i, n] = flags[block[i, n] + (i + shift) * at.blocks_per]

            up_to(live[i], find)


def listed(at, shift, block, live, with_places=False):
    out = [jax.ShapeDtypeStruct((at.size,), jnp.int32)]
    if with_places:
        out.append(jax.ShapeDtypeStruct(block.shape, jnp.int32))
    return pl.pallas_call(
        functools.partial(list_kernel, at, shift),
        out_shape=out,
        in_specs=[pl.BlockSpec(memory_space=pltpu.SMEM)] * 2,
        out_specs=[pl.BlockSpec(memory_space=pltpu.SMEM)] * len(out),
        scratch_shapes=[pltpu.SMEM((at.keys,), jnp.int32)],
        cost_estimate=LIGHT,
    )(live, block)


def pack_kernel(at, first, room, meta, *refs):
    borders, psi, out = refs[:-2], refs[-2], refs[-1]

    def one(c):
        key = jnp.where(first + c < meta[at.start + at.count + 1], meta[at.order + first + c], at.blocks_per)
        side, block = key // at.blocks_per, key % at.blocks_per
        for border in borders:

            @pl.when(side == 0)
            def _(border=border):
                out[:, lanes(c)] = border[:, lanes(block)]

        @pl.when(side > 0)
        def _():
            out[:, lanes(c)] = psi[side - 1, :, lanes(block)]

    up_to(room, one)


def pack(at, first, room, meta, psi, *borders):
    return pl.pallas_call(
        functools.partial(pack_kernel, at, first, room),
        out_shape=jax.ShapeDtypeStruct((psi.shape[1], room * EDGE), psi.dtype),
        in_specs=[pl.BlockSpec(memory_space=pltpu.SMEM)]
        + [pl.BlockSpec(memory_space=pltpu.VMEM)] * (1 + len(borders)),
        out_specs=pl.BlockSpec(memory_space=pltpu.VMEM),
        compiler_params=pltpu.CompilerParams(vmem_limit_bytes=8 * MIB),
        cost_estimate=LIGHT,
    )(meta, *borders, psi)


def coupling_kernel(at, room, many, meta, live, row, col, *refs):
    phis, (k_blocks, m_blocks, out, total) = refs[:many], refs[many:]
    i = pl.program_id(0)
    couple_one(at, room, i, meta, live, row, col, phis, k_blocks, m_blocks, out, total)


def couple_one(at, room, i, meta, live, row, col, phis, k_blocks, m_blocks, out, total):
    modes, blocks = phis[0].shape[1], phis[0].shape[2] // EDGE
    here, middle, end = (meta[at.start + i + n] for n in range(3))
    first = at.blocks_per * i

    def clear(n):
        total[meta[at.order + here + n] - first] = jnp.zeros(total.shape[1:], total.dtype)

    up_to(end - here, clear)

    def add_slots(step):
        terms = []
        for n in range(SLOTS):
            slot = jnp.minimum(step * SLOTS + n, at.slots - 1)
            where = row[i, slot]
            here = (step * SLOTS + n < live[i]) & (where >= 0) & (where < blocks)
            which = lanes(jnp.clip(where, 0, blocks - 1))
            picked = sum([phi[0, :, which] for phi in phis[1:]], phis[0][0, :, which])
            both = jnp.concatenate([k_blocks[0, slot], m_blocks[0, slot]], axis=1)
            to = jnp.where(here, col[i, slot], 2 * at.blocks_per)
            terms.append((to, jnp.dot(picked, both, preferred_element_type=jnp.float32)))
        for to, term in terms:
            total[to] += term

    up_to((live[i] + SLOTS - 1) // SLOTS, add_slots)

    def put(flavour, c):
        done = total[meta[at.order + c] - first].astype(out.dtype)
        out[flavour * ROWS : flavour * ROWS + modes, lanes(c)] = done[:, :EDGE]
        out[(flavour + 1) * ROWS : (flavour + 1) * ROWS + modes, lanes(c)] = done[:, EDGE:]

    def blank(top, c):
        out[top : top + 2 * ROWS, lanes(c)] = jnp.zeros((2 * ROWS, EDGE), out.dtype)

    up_to(middle - here, lambda n: put(2, here + n))
    up_to(end - middle, lambda n: put(0, middle + n))

    @pl.when(i == 0)
    def _():
        up_to(middle, lambda n: blank(0, n))

    @pl.when(i == at.count - 1)
    def _():
        up_to(room - middle, lambda n: blank(2 * ROWS, middle + n))
        up_to(room - end, lambda n: blank(0, end + n))


def couple(at, room, meta, live, row, col, phis, k_blocks, m_blocks, cost=LIGHT):
    _, modes, width = phis[0].shape
    count, slots = k_blocks.shape[:2]
    return pl.pallas_call(
        functools.partial(coupling_kernel, at, room, len(phis)),
        out_shape=jax.ShapeDtypeStruct((4 * ROWS, room * EDGE), phis[0].dtype),
        grid_spec=pltpu.PrefetchScalarGridSpec(
            num_scalar_prefetch=4,
            grid=(count,),
            in_specs=[
                pl.BlockSpec(
                    (1, modes, width), lambda i, *_, phi=phi: (0 if phi.shape[0] == 1 else i, 0, 0)
                )
                for phi in phis
            ]
            + [pl.BlockSpec((1, slots, EDGE, EDGE), lambda i, *_: (i, 0, 0, 0))] * 2,
            out_specs=pl.BlockSpec(
                (4 * ROWS, room * EDGE), lambda i, *_: (0, 0), pipeline_mode=pl.Buffered(1)
            ),
            scratch_shapes=[pltpu.VMEM((2 * at.blocks_per + 1, modes, 2 * EDGE), jnp.float32)],
        ),
        compiler_params=pltpu.CompilerParams(vmem_limit_bytes=56 * MIB),
        cost_estimate=cost,
    )(meta, live, row, col, *phis, k_blocks, m_blocks)


def sum_blocks(at, meta, bounds, coupling, shard, groups, right, total):
    low, high = bounds
    modes = shard.shape[1]

    def on_side(side):
        begin = jnp.maximum(meta[at.start + side], low)
        end = jnp.minimum(meta[at.start + side + 1], high)

        def bite(n):
            want = begin + n * BITE
            first = jnp.minimum(want, high - BITE)
            lane = lax.broadcasted_iota(jnp.int32, (modes, BITE * EDGE), 1) + first * EDGE
            inside = (lane >= want * EDGE) & (lane < end * EDGE)
            for g, group in enumerate(groups):
                part = shard[group[0], :, lanes(first, BITE)]
                for other in group[1:]:
                    part = part + shard[other, :, lanes(first, BITE)]
                part = jnp.where(inside, part, jnp.zeros_like(part))
                right[g * EDGE : g * EDGE + modes, :] = part
            total[side] += lax.dot_general(
                coupling[:, lanes(first, BITE)],
                right[...],
                (((1,), (1,)), ((), ())),
                preferred_element_type=jnp.float32,
            )

        up_to(jnp.maximum(end - begin + BITE - 1, 0) // BITE, bite)

    up_to(at.count + 1, on_side)


def put_products(at, groups, modes, total, out):
    for side in range(at.count + 1):
        for g in range(len(groups)):
            for flavour, (sub, part) in enumerate(
                ((side - 1, 1), (side - 1, 3), (side, 0), (side, 2))
            ):
                if 0 <= sub < at.count:
                    top, to = flavour * ROWS, (g * 4 + part) * modes
                    one = total[side, top : top + modes, g * EDGE : g * EDGE + modes]
                    out[sub, :, to : to + modes] = one.astype(out.dtype)


def grouped(sets):
    groups, taken = [], 0
    for size in sets:
        groups.append(range(taken, taken + size))
        taken += size
    return groups


def project_kernel(at, room, sets, meta, coupling, *refs):
    many = sum(sets)
    shards, refs = refs[:many], refs[many:]
    out, held, shard, right, total, held_done, shard_done = refs
    parts = [(0, room // 2), (room // 2, room)]
    coming = [[], []]
    for k, one in enumerate(shards):
        coming[0].append(pltpu.make_async_copy(one, shard.at[k], shard_done.at[k]))
    for n, (low, high) in enumerate(parts):
        to = pl.ds(low * EDGE, (high - low) * EDGE)
        coming[n].append(
            pltpu.make_async_copy(coupling.at[:, to], held.at[:, to], held_done.at[n])
        )
    for copy in coming[0] + coming[1]:
        copy.start()
    right[...] = jnp.zeros(right.shape, right.dtype)
    total[...] = jnp.zeros(total.shape, total.dtype)
    for bounds, here in zip(parts, coming):
        for copy in here:
            copy.wait()
        sum_blocks(at, meta, bounds, held, shard, grouped(sets), right, total)
    put_products(at, grouped(sets), shard.shape[1], total, out)


def project(at, meta, coupling, groups):
    flat = [shard for group in groups for shard in group]
    modes = flat[0].shape[0]
    sets = tuple(len(group) for group in groups)
    n, room = len(groups), coupling.shape[1] // EDGE
    wide = -(-n * 4 * modes // EDGE) * EDGE
    return pl.pallas_call(
        functools.partial(project_kernel, at, room, sets),
        out_shape=jax.ShapeDtypeStruct((at.count, modes, wide), coupling.dtype),
        in_specs=[pl.BlockSpec(memory_space=pltpu.SMEM)]
        + [pl.BlockSpec(memory_space=pltpu.HBM)] * (1 + len(flat)),
        out_specs=pl.BlockSpec(memory_space=pltpu.VMEM),
        scratch_shapes=[
            pltpu.VMEM(coupling.shape, coupling.dtype),
            pltpu.VMEM((len(flat), modes, coupling.shape[1]), coupling.dtype),
            pltpu.VMEM((n * EDGE, BITE * EDGE), coupling.dtype),
            pltpu.VMEM((at.count + 1, 4 * ROWS, n * EDGE), jnp.float32),
            pltpu.SemaphoreType.DMA((2,)),
            pltpu.SemaphoreType.DMA((len(flat),)),
        ],
        compiler_params=pltpu.CompilerParams(vmem_limit_bytes=56 * MIB),
        cost_estimate=LIGHT,
    )(meta, coupling, *flat)


def couple_end(at, meta, ints, places, phi_in, blocks):
    live, _, col = ints
    phis = [one[None] for one in phi_in]
    return couple(at, ROOM, meta, live, places, col, phis, *blocks, cost=HEAVY)


def assemble_kernel(modes, place, near, late, grid_k, grid_m, wide):
    own, left, right = ((near, g * 4 * modes) for g in range(3))
    second, third = ((late, g * (late.shape[2] // 2)) for g in range(2))
    plans = (
        (own, right, second, third),
        (left, own, right, second),
        (second, left, own, right),
        (third, second, left, own),
    )
    for which, grid in enumerate((grid_k, grid_m)):
        for z, plan in enumerate(plans):

            @pl.when(place[0] == z)
            def _(plan=plan, which=which):
                for far in range(2):
                    for h, (part, base) in enumerate(plan):
                        take = base + (2 * which + far) * modes
                        at = (4 * far + h) * modes
                        wide[:, :, at : at + modes] = part[:, :, take : take + modes].astype(
                            jnp.float32
                        )

        grid[...] = jnp.transpose(wide[...], (1, 0, 2))


def assemble(place, parts, modes):
    owners, rows, _ = parts[0].shape
    out = jax.ShapeDtypeStruct((rows, owners, 8 * modes), jnp.float32)
    group, tall = min(owners, 8), min(rows, TALL)
    block = pl.BlockSpec((tall, group, 8 * modes), lambda d, r, place: (r, d, 0))
    return pl.pallas_call(
        functools.partial(assemble_kernel, modes),
        out_shape=[out, out],
        grid_spec=pltpu.PrefetchScalarGridSpec(
            num_scalar_prefetch=1,
            grid=(owners // group, pl.cdiv(rows, tall)),
            in_specs=[
                pl.BlockSpec((group, tall, part.shape[2]), lambda d, r, place: (d, r, 0))
                for part in parts
            ],
            out_specs=[block] * 2,
            scratch_shapes=[pltpu.VMEM((group, tall, 8 * modes), jnp.float32)],
        ),
        compiler_params=pltpu.CompilerParams(vmem_limit_bytes=56 * MIB),
        cost_estimate=LIGHT,
    )(place, *parts)


def moved(shard, axis, by, sources=None):
    length = lax.axis_size(axis)
    sources = range(length) if sources is None else sources
    pairs = [(i, i + by) for i in sources if 0 <= i + by < length]
    return lax.ppermute(shard, axis, pairs)


def to_owners(part):
    count, modes, cols = part.shape
    owners = lax.axis_size("sub")
    part = part.reshape(owners, count * modes // owners, cols)
    return lax.all_to_all(part, "sub", split_axis=0, concat_axis=0, tiled=True)


def sent_in(phi_packed):
    last = lax.axis_size("grp") - 1
    return moved(phi_packed, "grp", 1, [0]), moved(phi_packed, "grp", -1, [last])


def sent_back(part):
    last = lax.axis_size("grp") - 1
    return lax.ppermute(part, "grp", [(1, 0), (last - 1, last)])


def both_ways(left, right):
    return moved(left, "grp", 1), moved(right, "grp", -1)


def main_path(at, lists, ints, phi, psi, border, blocks):
    meta, phi_meta, places, beside = lists
    modes = phi.shape[1]
    hold = lax.optimization_barrier

    own = pack(at, 0, ROOM, meta, psi, border)
    one = both_ways(own, own)
    own, phi, phi_meta = hold((own, phi, phi_meta))
    coupling = couple(at, ROOM, meta, *ints, [phi], *blocks)
    phi_in = sent_in(pack(at, 0, PHI_ROOM, phi_meta, phi))
    one, coupling, beside = hold((one, coupling, beside))
    last = lax.axis_size("grp") - 1
    two = (
        moved(one[0], "grp", 1, range(1, last)),
        moved(one[1], "grp", -1, range(last - 1, 0, -1)),
    )
    near = project(at, meta, coupling, [(own,), (one[0],), (one[1],)])
    near = to_owners(near)
    end = couple_end(at, meta, ints, places, phi_in, blocks)
    two, near, end = hold((two, near, end))
    third = project(at, meta, end, [two])
    third, far = hold((third, two))
    third = sent_back(third)
    second = project(at, meta, coupling, [far])
    third, second, near = hold((third, second, near))
    late = to_owners(jnp.concatenate([second, third], axis=2))
    place = lax.axis_index("grp").astype(jnp.int32)[None]
    return assemble(place, (near, late), modes), far, beside


def without(at, meta, by, room):
    kept = jnp.concatenate([meta[: at.start], jnp.full((at.start,), at.blocks_per, jnp.int32)])
    order = lax.dynamic_slice_in_dim(kept, by, at.start, 0)
    return jnp.concatenate([order, jnp.clip(meta[at.start :] - by, 0, room)])


def columns(part, modes, groups):
    part = part[:, :, : groups * 4 * modes].astype(jnp.float32)
    part = part.reshape(*part.shape[:2], groups, 2, 2, modes).transpose(3, 1, 0, 4, 2, 5)
    return part.reshape(2, *part.shape[1:3], 2 * groups * modes)


def add_kernel(old, new, out):
    out[...] = old[...] + new[...]


def added(old, new):
    rows, owners, cols = old.shape
    block = pl.BlockSpec((rows, min(owners, 8), cols), lambda d: (0, d, 0))
    return pl.pallas_call(
        add_kernel,
        out_shape=jax.ShapeDtypeStruct(old.shape, old.dtype),
        grid=(owners // min(owners, 8),),
        in_specs=[block, block],
        out_specs=block,
        input_output_aliases={0: 0},
        compiler_params=pltpu.CompilerParams(vmem_limit_bytes=32 * MIB),
    )(old, new)


def per_device(phi, psi, k_blocks, m_blocks, block_row, block_col, live):
    count, modes, width = phi.shape
    at = Meta(count, k_blocks.shape[1], width // EDGE)
    blocks = (k_blocks, m_blocks)
    ints = (live, block_row, block_col)
    border = moved(psi[count - 1], "sub", 1)
    (whole,) = listed(at, 0, block_col, live)
    phi_whole, places = listed(at, 1, block_row, live, with_places=True)
    total = at.start + count + 1
    most = lax.pmax(jnp.stack([whole[total], phi_whole[total]]), "sub")
    meta = jnp.concatenate([whole[: at.start], jnp.minimum(whole[at.start :], ROOM)])
    lists = (meta, phi_whole, places, most)
    grids, far, most = main_path(at, lists, ints, phi, psi, border, blocks)

    def turned(whole):
        return whole.transpose(1, 0, 2)

    def more(state):
        n, phi, psi, far, before = state[0], state[1], state[2], state[3], state[4:]
        phi, psi, far = lax.optimization_barrier((phi, psi, far))
        phi, psi = turned(phi), turned(psi)

        rest = without(at, whole, ROOM + n * MORE, MORE)
        packed = pack(at, 0, MORE, rest, psi, border)
        packed = jnp.stack([packed] * lax.axis_size("grp"))
        packed = lax.all_to_all(packed, "grp", split_axis=0, concat_axis=0, tiled=True)
        coupling = couple(at, MORE, rest, *ints, [phi], *blocks)
        shards = [(packed[h],) for h in range(packed.shape[0])]
        part = to_owners(project(at, rest, coupling, shards))
        after = columns(part, modes, len(shards))

        skipped = (n + 1) * PHI_ROOM
        rest = without(at, phi_whole, skipped, PHI_ROOM)
        phi_in = sent_in(pack(at, 0, PHI_ROOM, rest, phi))
        end = couple_end(at, meta, ints, places - skipped, phi_in, blocks)
        part = project(at, meta, end, [far])
        part = columns(to_owners(sent_back(part)), modes, 1)
        place, zero = lax.axis_index("grp"), jnp.zeros_like(part[..., :modes])
        last = lax.axis_size("grp") - 1
        ends = []
        for low in (0, modes):
            one = part[..., low : low + modes]
            for h in range(last + 1):
                wanted = ((place == 0) & (h == last)) | ((place == last) & (h == 0))
                ends.append(jnp.where(wanted, one, zero))
        after = after + jnp.concatenate(ends, axis=-1)
        return (n + 1, *state[1:4], *(added(old, new) for old, new in zip(before, after)))

    def unfinished(state):
        psi_left = ROOM + state[0] * MORE < most[0]
        return psi_left | ((state[0] + 1) * PHI_ROOM < most[1])

    state = (jnp.int32(0), turned(phi), turned(psi), far, *grids)
    state = lax.while_loop(unfinished, more, state)
    return tuple(turned(grid)[None, None] for grid in state[4:])


def solution(mesh):
    placed = (
        P("sub", "grp", None),
        P("sub", "grp", None),
        P("sub", None, None, None),
        P("sub", None, None, None),
        P("sub", None),
        P("sub", None),
        P("sub"),
    )
    return jax.shard_map(
        per_device,
        mesh=mesh,
        in_specs=placed,
        out_specs=(P("sub", "grp", None, None, None), P("sub", "grp", None, None, None)),
        check_vma=False,
    )
```

time: 231 us -> 217 us (0.939)
  waiting for transfers between devices: 80.8 us -> 40.1 us
  Pallas kernels: 60.4 us -> 91.7 us
  starting transfers between devices: 58.6 us -> 45.2 us
  other arithmetic: 0.15 us -> 4.08 us
    ppermute x13 -> x7, waiting for transfers between devices: 64 us -> 16.2 us  [moved(): return lax.ppermute(shard, axis, pairs)]
    pallas_call x4 -> x7, Pallas kernels: 48.4 us -> 75 us  [the longest x3 36 us: project(): pl.pallas_call(functools.partial(project_kernel, at, room, sets), out_sha...]
    ppermute x13 -> x7, starting transfers between devices: 36.3 us -> 20.4 us  [moved(): return lax.ppermute(shard, axis, pairs)]
    ppermute x0 -> x1, waiting for transfers between devices: none -> 5.09 us  [sent_back(): return lax.ppermute(part, 'grp', [(1, 0), (last - 1, last)])]
    pallas_call x2, Pallas kernels: 5.58 us -> 9.93 us  [pack(): pl.pallas_call(functools.partial(pack_kernel, at, first, room), out_shape...]
    concatenate x0 -> x1, other arithmetic: none -> 2.59 us  [main_path(): late = to_owners(jnp.concatenate([second, third], axis=2))]
    unnamed x28 -> x14, local copies, waits for them, and re-layouts: 9.14 us -> 7.48 us
    optimization_barrier x1 -> x3, local copies, waits for them, and re-layouts: 5.43 us -> 5.37 us  [the longest x1 3.73 us: main_path(): own, phi, phi_meta = hold((own, phi, phi_meta))]
  transfers between devices with their start and end apart: 15 -> 10, of which waited for: 8 -> 3; matrix products, arithmetic and copies ran while one was open for 4% -> 5% of each run, Pallas kernels for 16% -> 32%
where the time goes in v2:
time: 217 us; the launch traced here: 214 us
  Pallas kernels  91.7 us (42%)
  starting transfers between devices  45.2 us (21%)
  waiting for transfers between devices  40.1 us (18%)
  local copies, waits for them, and re-layouts  16.2 us (7%)
  blocking collectives  14.3 us (7%)
  other arithmetic  4.08 us (2%)
    pallas_call x3, Pallas kernels, project(): pl.pallas_call(functools.partial(project_kernel, at, room, sets), out_sha...  36 us
    pallas_call x2, Pallas kernels, couple(): pl.pallas_call(functools.partial(coupling_kernel, at, room, len(phis)), o...  34 us
    all_to_all x2, starting transfers between devices, to_owners(): return lax.all_to_all(part, 'sub', split_axis=0, concat_axis=0, tiled=True)  23.6 us
    ppermute x7, starting transfers between devices, moved(): return lax.ppermute(shard, axis, pairs)  20.4 us
    all_to_all x2, waiting for transfers between devices, to_owners(): return lax.all_to_all(part, 'sub', split_axis=0, concat_axis=0, tiled=True)  18.8 us
    ppermute x7, waiting for transfers between devices, moved(): return lax.ppermute(shard, axis, pairs)  16.2 us
    pmax x1, blocking collectives, per_device(): most = lax.pmax(jnp.stack([whole[total], phi_whole[total]]), 'sub')  14.3 us
    pallas_call x2, Pallas kernels, pack(): pl.pallas_call(functools.partial(pack_kernel, at, first, room), out_shape...  9.93 us
  transfers between devices with their start and end apart: 10, of which 3 were waited for; matrix products, arithmetic and copies ran while one was open for 5% of the time, Pallas kernels for 32%

profile of v2, /device:TPU:0, one launch (start us, length us, event | category | flops | bytes accessed | tf_op | source)
XLA Modules:
  0.0 213.9 jit_solution(16316349485713041399)
XLA Ops:
  0.7 3.7 %copy.80.refs_1_ = bf16[8,100,2048]{2,1,0:T(8,128)(2,1)S(1)} copy(bf16[8,100,2048]{2,0,1:T(8,128)(2,1)} %param.10) | data formatting | bytes 6553600 | tf_op args[1]
  5.3 3.1 %collective-permute-start.3 = (bf16[100,2048]{1,0:T(8,128)(2,1)}, bf16[100,2048]{1,0:T(8,128)(2,1)}, u32[]{:S(2)}, u32[]{:S(2)}) collective-permute-start(bf16[100,2048]{1,0:T(8,128)(2,1)} %slice_bitcast_fusion.6), channel_id=1, source_target_pairs={{0,4},{4,8},{8,12},{12,16},{16,20},{20,24},{24,28},{1,5},{5,9},{9,... | collective-permute-start | bytes 1228808 | tf_op jit(solution)/shard_map/ppermute | solution.py:359
  10.6 5.4 %shard_map.87.refs_0_ = bf16[100,11264]{1,0:T(8,128)(2,1)} custom-call(s32[330]{0:T(512)S(1)} %pad_add_fusion.2.meta, bf16[100,2048]{1,0:T(8,128)(2,1)} %collective-permute-done.3.refs_0_, bf16[8,100,2048]{2,1,0:T(8,128)(2,1)S(1)} %copy.80.refs_1_), custom_call_target="tpu_custom_call" | custom-call | flops 1 | bytes 1 | tf_op jit(solution)/shard_map/pallas_call | solution.py:111
  16.1 5.8 %collective-permute-start.4 = (bf16[100,11264]{1,0:T(8,128)(2,1)}, bf16[100,11264]{1,0:T(8,128)(2,1)}, u32[]{:S(2)}, u32[]{:S(2)}) collective-permute-start(bf16[100,11264]{1,0:T(8,128)(2,1)} %shard_map.87.refs_0_), channel_id=1, source_target_pairs={{0,1},{1,2},{2,3},{4,5},{5,6},{6,7},{8,9},{9,10},{10,11},{12,13},{... | collective-permute-start | bytes 6758408 | tf_op jit(solution)/shard_map/ppermute | solution.py:359
  23.1 2.9 %shard_map.88 = (s32[330]{0:T(512)S(1)}, s32[8,24]{1,0:T(8,128)S(1)}) custom-call(s32[8]{0:T(128)S(1)} %copy-done.14, s32[8,24]{1,0:T(8,128)S(1)} %copy-done.12), custom_call_target="tpu_custom_call" | custom-call | flops 1 | bytes 1 | tf_op jit(solution)/shard_map/pallas_call | solution.py:81
  26.0 3.7 %copy.64.refs_0_ = bf16[8,100,2048]{2,1,0:T(8,128)(2,1)S(1)} copy(bf16[8,100,2048]{2,0,1:T(8,128)(2,1)} %param.9) | data formatting | bytes 6553600 | tf_op jit(solution)/shard_map/optimization_barrier | solution.py:390
  29.8 4.5 %shard_map.91 = bf16[100,11264]{1,0:T(8,128)(2,1)} custom-call(s32[330]{0:T(512)S(1)} %get-tuple-element.471.meta, bf16[8,100,2048]{2,1,0:T(8,128)(2,1)S(1)} %copy.64.refs_0_), custom_call_target="tpu_custom_call" | custom-call | flops 1 | bytes 1 | tf_op jit(solution)/shard_map/pallas_call | solution.py:111
  34.3 6.0 %collective-permute-start.8 = (bf16[100,11264]{1,0:T(8,128)(2,1)}, bf16[100,11264]{1,0:T(8,128)(2,1)}, u32[]{:S(2)}, u32[]{:S(2)}) collective-permute-start(bf16[100,11264]{1,0:T(8,128)(2,1)} %shard_map.91), channel_id=1, source_target_pairs={{0,1},{4,5},{8,9},{12,13},{16,17},{20,21},{24,25},{28,29}} | collective-permute-start | bytes 6758408 | tf_op jit(solution)/shard_map/ppermute | solution.py:359
  40.2 2.1 collective-permute-start.9
  45.0 14.3 %pmax.7 = s32[2]{0:T(128)} all-reduce(s32[2]{0:T(128)S(1)} %pad_add_fusion.3), channel_id=1, replica_groups=mesh['sub'=8,'grp'=4] {'sub'}, use_global_device_ids=true, to_apply=%region_0.0 | all-reduce | flops 2 | bytes 16 | tf_op jit(solution)/shard_map/pmax | solution.py:452
  59.3 16.4 %shard_map.89.coupling = bf16[448,11264]{1,0:T(8,128)(2,1)} custom-call(s32[330]{0:T(512)S(1)} %pad_add_fusion.2.meta, s32[8]{0:T(128)S(1)} %copy-done.14, s32[8,24]{1,0:T(8,128)S(1)} %copy-done.12, s32[8,24]{1,0:T(8,128)S(1)} %copy-done.13, bf16[8,100,2048]{2,1,0:T(8,128)(2,1)} %copy-done, bf16[8,24,128,128]{3,2,1,0:T(8,128)(2,1)} %refs_2_.3, ...), custom_call_target="tpu_custom_call" | custom-call | flops 1 | bytes 1 | tf_op jit(solution)/shard_map/pallas_call | solution.py:178
  77.8 15.0 %shard_map.90 = bf16[8,100,1280]{2,1,0:T(8,128)(2,1)} custom-call(s32[330]{0:T(512)S(1)} %pad_add_fusion.2.meta, bf16[448,11264]{1,0:T(8,128)(2,1)} %shard_map.89.coupling, bf16[100,11264]{1,0:T(8,128)(2,1)} %shard_map.87.refs_0_, bf16[100,11264]{1,0:T(8,128)(2,1)} %collective-permute-done.4.refs_1_, bf16[100,11264]{1,0:T(8,128)(2,1)} %collective-permute-done.5.refs_2_), custom_call_target="tpu_custom_call" | custom-call | flops 1 | bytes 1 | tf_op jit(solution)/shard_map/pallas_call | solution.py:282
  92.8 9.9 %all-to-all-start.3 = ((bf16[8,100,1280]{2,1,0:T(8,128)(2,1)}), bf16[8,100,1280]{2,1,0:T(8,128)(2,1)}, u32[]{:S(2)}, u32[]{:S(2)}) async-start(bf16[8,100,1280]{2,1,0:T(8,128)(2,1)} %shard_map.90), calls=%async_computation.3 | async-start | bytes 4259840 | tf_op jit(solution)/shard_map/all_to_all | solution.py:366
  102.7 16.2 %collective-permute-done.8 = bf16[100,11264]{1,0:T(8,128)(2,1)} collective-permute-done((bf16[100,11264]{1,0:T(8,128)(2,1)}, bf16[100,11264]{1,0:T(8,128)(2,1)}, u32[]{:S(2)}, u32[]{:S(2)}) %collective-permute-start.8) | collective-permute-done | bytes 2252832 | tf_op jit(solution)/shard_map/ppermute | solution.py:359
  119.0 17.6 %shard_map.92.coupling = bf16[448,11264]{1,0:T(8,128)(2,1)} custom-call(s32[330]{0:T(512)S(1)} %pad_add_fusion.2.meta, s32[8]{0:T(128)S(1)} %copy-done.14, s32[8,24]{1,0:T(8,128)S(1)} %get-tuple-element.694.row, s32[8,24]{1,0:T(8,128)S(1)} %copy-done.13, bf16[1,100,11264]{2,1,0:T(8,128)(2,1)} %bitcast.21.refs_0_, bf16[1,100,11264]{2,1,0:T(8,128)(2,1)} %bitcast.22.refs_1_, ...), custom_call_target="tpu_custom_call" | custom-call | flops 24999999488 | bytes 1 | tf_op jit(solution)/shard_map/pallas_call | solution.py:178
  136.6 10.5 %shard_map.93 = bf16[8,100,512]{2,1,0:T(8,128)(2,1)} custom-call(s32[330]{0:T(512)S(1)} %pad_add_fusion.2.meta, bf16[448,11264]{1,0:T(8,128)(2,1)} %shard_map.92.coupling, bf16[100,11264]{1,0:T(8,128)(2,1)S(1)} %collective-permute-done.6.refs_0_, bf16[100,11264]{1,0:T(8,128)(2,1)} %collective-permute-done.7.refs_1_), custom_call_target="tpu_custom_call" | custom-call | flops 1 | bytes 1 | tf_op jit(solution)/shard_map/pallas_call | solution.py:282
  149.8 10.5 %shard_map.94 = bf16[8,100,512]{2,1,0:T(8,128)(2,1)} custom-call(s32[330]{0:T(512)S(1)} %pad_add_fusion.2.meta, bf16[448,11264]{1,0:T(8,128)(2,1)} %shard_map.89.coupling, bf16[100,11264]{1,0:T(8,128)(2,1)S(1)} %collective-permute-done.6.refs_0_, bf16[100,11264]{1,0:T(8,128)(2,1)} %collective-permute-done.7.refs_1_), custom_call_target="tpu_custom_call" | custom-call | flops 1 | bytes 1 | tf_op jit(solution)/shard_map/pallas_call | solution.py:282
  160.3 5.1 %collective-permute-done.10 = bf16[8,100,512]{2,0,1:T(8,128)(2,1)S(1)} collective-permute-done((bf16[8,100,512]{2,0,1:T(8,128)(2,1)S(1)}, bf16[8,100,512]{2,0,1:T(8,128)(2,1)S(1)}, u32[]{:S(2)}, u32[]{:S(2)}) %collective-permute-start.10) | collective-permute-done | bytes 819232 | tf_op jit(solution)/shard_map/ppermute | solution.py:376
  165.7 2.6 %pad_maximum_fusion = bf16[8,100,1024]{2,1,0:T(8,128)(2,1)} fusion(bf16[8,100,512]{2,1,0:T(8,128)(2,1)S(1)} %copy.67, bf16[8,100,512]{2,1,0:T(8,128)(2,1)} %shard_map.94), kind=kLoop, calls=%fused_computation.19 | loop fusion | flops 3276800 | bytes 3276800 | tf_op jit(solution)/shard_map/concatenate | solution.py:408
  168.3 13.7 %all-to-all-start.4 = ((bf16[8,100,1024]{2,1,0:T(8,128)(2,1)}), bf16[8,100,1024]{2,1,0:T(8,128)(2,1)}, u32[]{:S(2)}, u32[]{:S(2)}) async-start(bf16[8,100,1024]{2,1,0:T(8,128)(2,1)} %pad_maximum_fusion), calls=%async_computation.4 | async-start | bytes 3407872 | tf_op jit(solution)/shard_map/all_to_all | solution.py:366
  181.9 3.7 %copy.79 = bf16[8,100,2048]{2,1,0:T(8,128)(2,1)S(1)} copy(bf16[8,100,2048]{2,0,1:T(8,128)(2,1)} %param.9) | data formatting | bytes 6553600 | tf_op args[0]
  185.7 18.8 %all-to-all-done.4.late = bf16[8,100,1024]{2,1,0:T(8,128)(2,1)} async-done(((bf16[8,100,1024]{2,1,0:T(8,128)(2,1)}), bf16[8,100,1024]{2,1,0:T(8,128)(2,1)}, u32[]{:S(2)}, u32[]{:S(2)}) %all-to-all-start.4) | async-done | bytes 1638432 | tf_op jit(solution)/shard_map/all_to_all | solution.py:366
  204.5 6.8 %shard_map.95 = (f32[100,8,800]{2,1,0:T(8,128)}, f32[100,8,800]{2,1,0:T(8,128)}) custom-call(s32[1]{0:T(128)} %bitcast.19.place, bf16[8,100,1280]{2,1,0:T(8,128)(2,1)} %all-to-all-done.3.near, bf16[8,100,1024]{2,1,0:T(8,128)(2,1)} %all-to-all-done.4.late), custom_call_target="tpu_custom_call" | custom-call | flops 1 | bytes 1 | tf_op jit(solution)/shard_map/pallas_call | solution.py:337
  211.2 2.5 %while.16 = (s32[]{:T(128)}, f32[100,8,800]{2,1,0:T(8,128)}, f32[100,8,800]{2,1,0:T(8,128)}, s32[2]{0:T(128)}, s32[330]{0:T(512)S(1)}, /*index=5*/bf16[100,8,204...) while((s32[]{:T(128)}, f32[100,8,800]{2,1,0:T(8,128)}, ...), condition=%wide.region_2.3_spmd, body=%wide.region_1.2_spmd.sunk | while | flops 25003517952 | bytes 222021552 | solution.py:496
  (33 shorter events, 13.3 us)
Async XLA Ops:
  0.6 7.7 %copy-start.13 = (s32[8,24]{1,0:T(8,128)S(1)}, s32[8,24]{1,0:T(8,128)}, u32[]{:S(2)}) copy-start(s32[8,24]{1,0:T(8,128)} %col.3) | copy-start | bytes 2308
  0.6 7.7 %copy-start.14 = (s32[8]{0:T(128)S(1)}, s32[8]{0:T(128)}, u32[]{:S(2)}) copy-start(s32[8]{0:T(128)} %live.7) | copy-start | bytes 100
  4.4 11.7 %copy-start.5 = (bf16[8,100,2048]{2,1,0:T(8,128)(2,1)}, bf16[8,100,2048]{2,1,0:T(8,128)(2,1)S(1)}, u32[]{:S(2)}) copy-start(bf16[8,100,2048]{2,1,0:T(8,128)(2,1)S(1)} %copy.80.refs_1_) | copy-start | bytes 9830404
  5.3 5.4 %collective-permute-start.3 = (bf16[100,2048]{1,0:T(8,128)(2,1)}, bf16[100,2048]{1,0:T(8,128)(2,1)}, u32[]{:S(2)}, u32[]{:S(2)}) collective-permute-start(bf16[100,2048]{1,0:T(8,128)(2,1)} %slice_bitcast_fusion.6), channel_id=1, source_target_pairs={{0,4},{4,8},{8,12},{12,16},{16,20},{20,24},{24,28},{1,5},{5,9},{9,... | collective-permute-start | bytes 1228808 | tf_op jit(solution)/shard_map/ppermute | solution.py:359
  10.6 12.5 %copy-start.12 = (s32[8,24]{1,0:T(8,128)S(1)}, s32[8,24]{1,0:T(8,128)}, u32[]{:S(2)}) copy-start(s32[8,24]{1,0:T(8,128)} %row.1) | copy-start | bytes 2308
  16.1 59.6 %collective-permute-start.4 = (bf16[100,11264]{1,0:T(8,128)(2,1)}, bf16[100,11264]{1,0:T(8,128)(2,1)}, u32[]{:S(2)}, u32[]{:S(2)}) collective-permute-start(bf16[100,11264]{1,0:T(8,128)(2,1)} %shard_map.87.refs_0_), channel_id=1, source_target_pairs={{0,1},{1,2},{2,3},{4,5},{5,6},{6,7},{8,9},{9,10},{10,11},{12,13},{... | collective-permute-start | bytes 6758408 | tf_op jit(solution)/shard_map/ppermute | solution.py:359
  21.8 53.9 %collective-permute-start.5 = (bf16[100,11264]{1,0:T(8,128)(2,1)}, bf16[100,11264]{1,0:T(8,128)(2,1)}, u32[]{:S(2)}, u32[]{:S(2)}) collective-permute-start(bf16[100,11264]{1,0:T(8,128)(2,1)} %shard_map.87.refs_0_), channel_id=1, source_target_pairs={{1,0},{2,1},{3,2},{5,4},{6,5},{7,6},{9,8},{10,9},{11,10},{13,12},{... | collective-permute-start | bytes 6758408 | tf_op jit(solution)/shard_map/ppermute | solution.py:359
  29.7 4.5 %copy-start = (bf16[8,100,2048]{2,1,0:T(8,128)(2,1)}, bf16[8,100,2048]{2,1,0:T(8,128)(2,1)S(1)}, u32[]{:S(2)}) copy-start(bf16[8,100,2048]{2,1,0:T(8,128)(2,1)S(1)} %copy.64.refs_0_) | copy-start | bytes 9830404
  34.3 84.7 %collective-permute-start.8 = (bf16[100,11264]{1,0:T(8,128)(2,1)}, bf16[100,11264]{1,0:T(8,128)(2,1)}, u32[]{:S(2)}, u32[]{:S(2)}) collective-permute-start(bf16[100,11264]{1,0:T(8,128)(2,1)} %shard_map.91), channel_id=1, source_target_pairs={{0,1},{4,5},{8,9},{12,13},{16,17},{20,21},{24,25},{28,29}} | collective-permute-start | bytes 6758408 | tf_op jit(solution)/shard_map/ppermute | solution.py:359
  40.2 78.7 %collective-permute-start.9 = (bf16[100,11264]{1,0:T(8,128)(2,1)}, bf16[100,11264]{1,0:T(8,128)(2,1)}, u32[]{:S(2)}, u32[]{:S(2)}) collective-permute-start(bf16[100,11264]{1,0:T(8,128)(2,1)} %shard_map.91), channel_id=1, source_target_pairs={{3,2},{7,6},{11,10},{15,14},{19,18},{23,22},{27,26},{31,30}} | collective-permute-start | bytes 6758408 | tf_op jit(solution)/shard_map/ppermute | solution.py:359
  75.7 60.8 %collective-permute-start.6 = (bf16[100,11264]{1,0:T(8,128)(2,1)}, bf16[100,11264]{1,0:T(8,128)(2,1)S(1)}, u32[]{:S(2)}, u32[]{:S(2)}) collective-permute-start(bf16[100,11264]{1,0:T(8,128)(2,1)} %collective-permute-done.4.refs_1_), channel_id=1, source_target_pairs={{1,2},{2,3},{5,6},{6,7},{9,10},{10,11},{13,14},{14,15},{17,18},{18... | collective-permute-start | bytes 6758408 | tf_op jit(solution)/shard_map/ppermute | solution.py:359
  76.5 60.0 %collective-permute-start.7 = (bf16[100,11264]{1,0:T(8,128)(2,1)}, bf16[100,11264]{1,0:T(8,128)(2,1)}, u32[]{:S(2)}, u32[]{:S(2)}) collective-permute-start(bf16[100,11264]{1,0:T(8,128)(2,1)} %collective-permute-done.5.refs_2_), channel_id=1, source_target_pairs={{2,1},{1,0},{6,5},{5,4},{10,9},{9,8},{14,13},{13,12},{18,17},{17,1... | collective-permute-start | bytes 6758408 | tf_op jit(solution)/shard_map/ppermute | solution.py:359
  92.8 43.7 %all-to-all-start.3 = ((bf16[8,100,1280]{2,1,0:T(8,128)(2,1)}), bf16[8,100,1280]{2,1,0:T(8,128)(2,1)}, u32[]{:S(2)}, u32[]{:S(2)}) async-start(bf16[8,100,1280]{2,1,0:T(8,128)(2,1)} %shard_map.90), calls=%async_computation.3 | async-start | bytes 4259840 | tf_op jit(solution)/shard_map/all_to_all | solution.py:366
  136.6 13.2 %copy-start.6 = (bf16[100,11264]{1,0:T(8,128)(2,1)}, bf16[100,11264]{1,0:T(8,128)(2,1)S(1)}, u32[]{:S(2)}) copy-start(bf16[100,11264]{1,0:T(8,128)(2,1)S(1)} %collective-permute-done.6.refs_0_) | copy-start | bytes 6758404
  148.5 16.9 %collective-permute-start.10 = (bf16[8,100,512]{2,0,1:T(8,128)(2,1)S(1)}, bf16[8,100,512]{2,0,1:T(8,128)(2,1)S(1)}, u32[]{:S(2)}, u32[]{:S(2)}) collective-permute-start(bf16[8,100,512]{2,0,1:T(8,128)(2,1)S(1)} %copy.66), channel_id=1, source_target_pairs={{1,0},{2,3},{5,4},{6,7},{9,8},{10,11},{13,12},{14,15},{17,16},{18,... | collective-permute-start | bytes 2457608 | tf_op jit(solution)/shard_map/ppermute | solution.py:376
  168.3 36.2 %all-to-all-start.4 = ((bf16[8,100,1024]{2,1,0:T(8,128)(2,1)}), bf16[8,100,1024]{2,1,0:T(8,128)(2,1)}, u32[]{:S(2)}, u32[]{:S(2)}) async-start(bf16[8,100,1024]{2,1,0:T(8,128)(2,1)} %pad_maximum_fusion), calls=%async_computation.4 | async-start | bytes 3407872 | tf_op jit(solution)/shard_map/all_to_all | solution.py:366

commit v3 on v2

--- a/solution.py
+++ b/solution.py
@@ -11,8 +11,8 @@
 ROWS = 112
 SLOTS = 4
 BITE = 4
-ROOM = 88
-PHI_ROOM = 88
+ROOM = 94
+PHI_ROOM = 92
 MORE = 16
 TALL = 32
 MIB = 1 << 20
@@ -90,21 +90,23 @@
 
 def pack_kernel(at, first, room, meta, *refs):
     borders, psi, out = refs[:-2], refs[-2], refs[-1]
-
-    def one(c):
-        key = jnp.where(first + c < meta[at.start + at.count + 1], meta[at.order + first + c], at.blocks_per)
-        side, block = key // at.blocks_per, key % at.blocks_per
+    split = jnp.clip(meta[at.start + 1] - first, 0, room)
+    end = jnp.clip(meta[at.start + at.count + 1] - first, 0, room)
+
+    def from_border(c):
         for border in borders:
-
-            @pl.when(side == 0)
-            def _(border=border):
-                out[:, lanes(c)] = border[:, lanes(block)]
-
-        @pl.when(side > 0)
-        def _():
-            out[:, lanes(c)] = psi[side - 1, :, lanes(block)]
-
-    up_to(room, one)
+            out[:, lanes(c)] = border[:, lanes(meta[at.order + first + c])]
+
+    def from_psi(c):
+        key = meta[at.order + first + c]
+        out[:, lanes(c)] = psi[key // at.blocks_per - 1, :, lanes(key % at.blocks_per)]
+
+    def from_none(c):
+        out[:, lanes(c)] = jnp.zeros((out.shape[0], EDGE), out.dtype)
+
+    up_to(split, from_border)
+    up_to(end - split, lambda c: from_psi(split + c))
+    up_to(room - end, lambda c: from_none(end + c))
 
 
 def pack(at, first, room, meta, psi, *borders):
@@ -198,7 +200,7 @@
     )(meta, live, row, col, *phis, k_blocks, m_blocks)
 
 
-def sum_blocks(at, meta, bounds, coupling, shard, groups, right, total):
+def sum_blocks(at, meta, bounds, couplings, shard, groups, right, totals):
     low, high = bounds
     modes = shard.shape[1]
 
@@ -217,12 +219,13 @@
                     part = part + shard[other, :, lanes(first, BITE)]
                 part = jnp.where(inside, part, jnp.zeros_like(part))
                 right[g * EDGE : g * EDGE + modes, :] = part
-            total[side] += lax.dot_general(
-                coupling[:, lanes(first, BITE)],
-                right[...],
-                (((1,), (1,)), ((), ())),
-                preferred_element_type=jnp.float32,
-            )
+            for coupling, total in zip(couplings, totals):
+                total[side] += lax.dot_general(
+                    coupling[:, lanes(first, BITE)],
+                    right[...],
+                    (((1,), (1,)), ((), ())),
+                    preferred_element_type=jnp.float32,
+                )
 
         up_to(jnp.maximum(end - begin + BITE - 1, 0) // BITE, bite)
 
@@ -249,53 +252,57 @@
     return groups
 
 
-def project_kernel(at, room, sets, meta, coupling, *refs):
-    many = sum(sets)
-    shards, refs = refs[:many], refs[many:]
-    out, held, shard, right, total, held_done, shard_done = refs
+def project_kernel(at, room, sets, many, meta, *refs):
+    couplings, refs = refs[:many], refs[many:]
+    shards, refs = refs[: sum(sets)], refs[sum(sets) :]
+    outs, refs = refs[:many], refs[many:]
+    helds, totals, (shard, right, held_done, shard_done) = refs[:many], refs[many : 2 * many], refs[2 * many :]
     parts = [(0, room // 2), (room // 2, room)]
     coming = [[], []]
     for k, one in enumerate(shards):
         coming[0].append(pltpu.make_async_copy(one, shard.at[k], shard_done.at[k]))
     for n, (low, high) in enumerate(parts):
         to = pl.ds(low * EDGE, (high - low) * EDGE)
-        coming[n].append(
-            pltpu.make_async_copy(coupling.at[:, to], held.at[:, to], held_done.at[n])
-        )
+        for k, (coupling, held) in enumerate(zip(couplings, helds)):
+            coming[n].append(
+                pltpu.make_async_copy(coupling.at[:, to], held.at[:, to], held_done.at[2 * k + n])
+            )
     for copy in coming[0] + coming[1]:
         copy.start()
     right[...] = jnp.zeros(right.shape, right.dtype)
-    total[...] = jnp.zeros(total.shape, total.dtype)
+    for total in totals:
+        total[...] = jnp.zeros(total.shape, total.dtype)
     for bounds, here in zip(parts, coming):
         for copy in here:
             copy.wait()
-        sum_blocks(at, meta, bounds, held, shard, grouped(sets), right, total)
-    put_products(at, grouped(sets), shard.shape[1], total, out)
-
-
-def project(at, meta, coupling, groups):
+        sum_blocks(at, meta, bounds, helds, shard, grouped(sets), right, totals)
+    for total, out in zip(totals, outs):
+        put_products(at, grouped(sets), shard.shape[1], total, out)
+
+
+def project(at, meta, couplings, groups):
     flat = [shard for group in groups for shard in group]
-    modes = flat[0].shape[0]
+    modes, held = flat[0].shape[0], couplings[0]
     sets = tuple(len(group) for group in groups)
-    n, room = len(groups), coupling.shape[1] // EDGE
+    n, many, room = len(groups), len(couplings), held.shape[1] // EDGE
     wide = -(-n * 4 * modes // EDGE) * EDGE
     return pl.pallas_call(
-        functools.partial(project_kernel, at, room, sets),
-        out_shape=jax.ShapeDtypeStruct((at.count, modes, wide), coupling.dtype),
+        functools.partial(project_kernel, at, room, sets, many),
+        out_shape=[jax.ShapeDtypeStruct((at.count, modes, wide), held.dtype)] * many,
         in_specs=[pl.BlockSpec(memory_space=pltpu.SMEM)]
-        + [pl.BlockSpec(memory_space=pltpu.HBM)] * (1 + len(flat)),
-        out_specs=pl.BlockSpec(memory_space=pltpu.VMEM),
-        scratch_shapes=[
-            pltpu.VMEM(coupling.shape, coupling.dtype),
-            pltpu.VMEM((len(flat), modes, coupling.shape[1]), coupling.dtype),
-            pltpu.VMEM((n * EDGE, BITE * EDGE), coupling.dtype),
-            pltpu.VMEM((at.count + 1, 4 * ROWS, n * EDGE), jnp.float32),
-            pltpu.SemaphoreType.DMA((2,)),
+        + [pl.BlockSpec(memory_space=pltpu.HBM)] * (many + len(flat)),
+        out_specs=[pl.BlockSpec(memory_space=pltpu.VMEM)] * many,
+        scratch_shapes=[pltpu.VMEM(held.shape, held.dtype)] * many
+        + [pltpu.VMEM((at.count + 1, 4 * ROWS, n * EDGE), jnp.float32)] * many
+        + [
+            pltpu.VMEM((len(flat), modes, held.shape[1]), held.dtype),
+            pltpu.VMEM((n * EDGE, BITE * EDGE), held.dtype),
+            pltpu.SemaphoreType.DMA((2 * many,)),
             pltpu.SemaphoreType.DMA((len(flat),)),
         ],
         compiler_params=pltpu.CompilerParams(vmem_limit_bytes=56 * MIB),
         cost_estimate=LIGHT,
-    )(meta, coupling, *flat)
+    )(meta, *couplings, *flat)
 
 
 def couple_end(at, meta, ints, places, phi_in, blocks):
@@ -304,9 +311,9 @@
     return couple(at, ROOM, meta, live, places, col, phis, *blocks, cost=HEAVY)
 
 
-def assemble_kernel(modes, place, near, late, grid_k, grid_m, wide):
+def assemble_kernel(modes, place, near, second, third, grid_k, grid_m, wide):
     own, left, right = ((near, g * 4 * modes) for g in range(3))
-    second, third = ((late, g * (late.shape[2] // 2)) for g in range(2))
+    second, third = (second, 0), (third, 0)
     plans = (
         (own, right, second, third),
         (left, own, right, second),
@@ -396,18 +403,17 @@
         moved(one[0], "grp", 1, range(1, last)),
         moved(one[1], "grp", -1, range(last - 1, 0, -1)),
     )
-    near = project(at, meta, coupling, [(own,), (one[0],), (one[1],)])
+    (near,) = project(at, meta, [coupling], [(own,), (one[0],), (one[1],)])
     near = to_owners(near)
     end = couple_end(at, meta, ints, places, phi_in, blocks)
     two, near, end = hold((two, near, end))
-    third = project(at, meta, end, [two])
-    third, far = hold((third, two))
+    second, third = project(at, meta, [coupling, end], [two])
     third = sent_back(third)
-    second = project(at, meta, coupling, [far])
+    second = to_owners(second)
     third, second, near = hold((third, second, near))
-    late = to_owners(jnp.concatenate([second, third], axis=2))
+    third = to_owners(third)
     place = lax.axis_index("grp").astype(jnp.int32)[None]
-    return assemble(place, (near, late), modes), far, beside
+    return assemble(place, (near, second, third), modes), two, beside
 
 
 def without(at, meta, by, room):
@@ -450,9 +456,12 @@
     phi_whole, places = listed(at, 1, block_row, live, with_places=True)
     total = at.start + count + 1
     most = lax.pmax(jnp.stack([whole[total], phi_whole[total]]), "sub")
+    over = jnp.maximum(most - jnp.asarray([ROOM, PHI_ROOM], jnp.int32), 0)
+    each = jnp.asarray([MORE, PHI_ROOM], jnp.int32)
+    trips = jnp.max((over + each - 1) // each)
     meta = jnp.concatenate([whole[: at.start], jnp.minimum(whole[at.start :], ROOM)])
-    lists = (meta, phi_whole, places, most)
-    grids, far, most = main_path(at, lists, ints, phi, psi, border, blocks)
+    lists = (meta, phi_whole, places, trips)
+    grids, far, trips = main_path(at, lists, ints, phi, psi, border, blocks)
 
     def turned(whole):
         return whole.transpose(1, 0, 2)
@@ -468,14 +477,14 @@
         packed = lax.all_to_all(packed, "grp", split_axis=0, concat_axis=0, tiled=True)
         coupling = couple(at, MORE, rest, *ints, [phi], *blocks)
         shards = [(packed[h],) for h in range(packed.shape[0])]
-        part = to_owners(project(at, rest, coupling, shards))
+        part = to_owners(project(at, rest, [coupling], shards)[0])
         after = columns(part, modes, len(shards))
 
         skipped = (n + 1) * PHI_ROOM
         rest = without(at, phi_whole, skipped, PHI_ROOM)
         phi_in = sent_in(pack(at, 0, PHI_ROOM, rest, phi))
         end = couple_end(at, meta, ints, places - skipped, phi_in, blocks)
-        part = project(at, meta, end, [far])
+        (part,) = project(at, meta, [end], [far])
         part = columns(to_owners(sent_back(part)), modes, 1)
         place, zero = lax.axis_index("grp"), jnp.zeros_like(part[..., :modes])
         last = lax.axis_size("grp") - 1
@@ -488,12 +497,8 @@
         after = after + jnp.concatenate(ends, axis=-1)
         return (n + 1, *state[1:4], *(added(old, new) for old, new in zip(before, after)))
 
-    def unfinished(state):
-        psi_left = ROOM + state[0] * MORE < most[0]
-        return psi_left | ((state[0] + 1) * PHI_ROOM < most[1])
-
     state = (jnp.int32(0), turned(phi), turned(psi), far, *grids)
-    state = lax.while_loop(unfinished, more, state)
+    state = lax.while_loop(lambda state: state[0] < trips, more, state)
     return tuple(turned(grid)[None, None] for grid in state[4:])
 
 

time: 217 us -> 217 us (level)
  blocking collectives: 14.3 us -> 38.2 us
  starting transfers between devices: 45.2 us -> 34.4 us
  waiting for transfers between devices: 40.1 us -> 29.6 us
    all_to_all x0 -> x1, blocking collectives: none -> 24.4 us  [to_owners(): return lax.all_to_all(part, 'sub', split_axis=0, concat_axis=0, tiled=True)]
    all_to_all x2, starting transfers between devices: 23.6 us -> 12.7 us  [to_owners(): return lax.all_to_all(part, 'sub', split_axis=0, concat_axis=0, tiled=True)]
    all_to_all x2, waiting for transfers between devices: 18.8 us -> 9.4 us  [to_owners(): return lax.all_to_all(part, 'sub', split_axis=0, concat_axis=0, tiled=True)]
    ppermute x1, waiting for transfers between devices: 5.09 us -> 0.01 us  [sent_back(): return lax.ppermute(part, 'grp', [(1, 0), (last - 1, last)])]
    ppermute x7, waiting for transfers between devices: 16.2 us -> 20.2 us  [moved(): return lax.ppermute(shard, axis, pairs)]
    concatenate x1 -> x0, other arithmetic: 2.59 us -> none  [main_path(): late = to_owners(jnp.concatenate([second, third], axis=2))]
    pallas_call x2, Pallas kernels: 9.93 us -> 7.49 us  [pack(): pl.pallas_call(functools.partial(pack_kernel, at, first, room), out_shape...]
    pallas_call x2, Pallas kernels: 34 us -> 36.4 us  [couple(): pl.pallas_call(functools.partial(coupling_kernel, at, room, len(phis)), o...]
  transfers between devices with their start and end apart: 10 -> 10, of which waited for: 3 -> 3; matrix products, arithmetic and copies ran while one was open for 5% -> 5% of each run, Pallas kernels for 32% -> 29%
where the time goes in v3:
time: 217 us; the launch traced here: 213 us
  Pallas kernels  91.4 us (42%)
  blocking collectives  38.2 us (18%)
  starting transfers between devices  34.4 us (16%)
  waiting for transfers between devices  29.6 us (14%)
  local copies, waits for them, and re-layouts  15.9 us (7%)
  other arithmetic  2.29 us (1%)
    pallas_call x2, Pallas kernels, couple(): pl.pallas_call(functools.partial(coupling_kernel, at, room, len(phis)), o...  36.4 us
    pallas_call x2, Pallas kernels, project(): pl.pallas_call(functools.partial(project_kernel, at, room, sets, many), o...  35.5 us
    all_to_all x1, blocking collectives, to_owners(): return lax.all_to_all(part, 'sub', split_axis=0, concat_axis=0, tiled=True)  24.4 us
    ppermute x7, starting transfers between devices, moved(): return lax.ppermute(shard, axis, pairs)  20.4 us
    ppermute x7, waiting for transfers between devices, moved(): return lax.ppermute(shard, axis, pairs)  20.2 us
    pmax x1, blocking collectives, per_device(): most = lax.pmax(jnp.stack([whole[total], phi_whole[total]]), 'sub')  13.9 us
    all_to_all x2, starting transfers between devices, to_owners(): return lax.all_to_all(part, 'sub', split_axis=0, concat_axis=0, tiled=True)  12.7 us
    all_to_all x2, waiting for transfers between devices, to_owners(): return lax.all_to_all(part, 'sub', split_axis=0, concat_axis=0, tiled=True)  9.4 us
  transfers between devices with their start and end apart: 10, of which 3 were waited for; matrix products, arithmetic and copies ran while one was open for 5% of the time, Pallas kernels for 29%

profile of v3, /device:TPU:0, one launch (start us, length us, event | category | flops | bytes accessed | tf_op | source)
XLA Modules:
  0.0 213.4 jit_solution(6849826512330332264)
XLA Ops:
  0.7 3.7 %copy.82.refs_1_ = bf16[8,100,2048]{2,1,0:T(8,128)(2,1)S(1)} copy(bf16[8,100,2048]{2,0,1:T(8,128)(2,1)} %param.12) | data formatting | bytes 6553600 | tf_op args[1]
  5.3 3.1 %collective-permute-start.3 = (bf16[100,2048]{1,0:T(8,128)(2,1)}, bf16[100,2048]{1,0:T(8,128)(2,1)}, u32[]{:S(2)}, u32[]{:S(2)}) collective-permute-start(bf16[100,2048]{1,0:T(8,128)(2,1)} %slice_bitcast_fusion.6), channel_id=1, source_target_pairs={{0,4},{4,8},{8,12},{12,16},{16,20},{20,24},{24,28},{1,5},{5,9},{9,... | collective-permute-start | bytes 1228808 | tf_op jit(solution)/shard_map/ppermute | solution.py:366
  8.4 2.2 %shard_map.104 = s32[338]{0:T(512)S(1)} custom-call(s32[8]{0:T(128)S(1)} %copy-done.14, s32[8,24]{1,0:T(8,128)S(1)} %copy-done.13), custom_call_target="tpu_custom_call" | custom-call | flops 1 | bytes 1 | tf_op jit(solution)/shard_map/pallas_call | solution.py:81
  10.7 4.0 %shard_map.105.refs_1_ = bf16[100,12032]{1,0:T(8,128)(2,1)} custom-call(s32[338]{0:T(512)S(1)} %pad_add_fusion.2.meta, bf16[100,2048]{1,0:T(8,128)(2,1)} %collective-permute-done.3.refs_0_, bf16[8,100,2048]{2,1,0:T(8,128)(2,1)S(1)} %copy.82.refs_1_), custom_call_target="tpu_custom_call" | custom-call | flops 1 | bytes 1 | tf_op jit(solution)/shard_map/pallas_call | solution.py:113
  14.7 5.8 %collective-permute-start.4 = (bf16[100,12032]{1,0:T(8,128)(2,1)}, bf16[100,12032]{1,0:T(8,128)(2,1)}, u32[]{:S(2)}, u32[]{:S(2)}) collective-permute-start(bf16[100,12032]{1,0:T(8,128)(2,1)} %shard_map.105.refs_1_), channel_id=1, source_target_pairs={{0,1},{1,2},{2,3},{4,5},{5,6},{6,7},{8,9},{9,10},{10,11},{12,13},{... | collective-permute-start | bytes 7219208 | tf_op jit(solution)/shard_map/ppermute | solution.py:366
  21.8 3.1 %shard_map.106 = (s32[338]{0:T(512)S(1)}, s32[8,24]{1,0:T(8,128)S(1)}) custom-call(s32[8]{0:T(128)S(1)} %copy-done.14, s32[8,24]{1,0:T(8,128)S(1)} %copy-done.12), custom_call_target="tpu_custom_call" | custom-call | flops 1 | bytes 1 | tf_op jit(solution)/shard_map/pallas_call | solution.py:81
  25.0 3.7 %copy.66.refs_0_ = bf16[8,100,2048]{2,1,0:T(8,128)(2,1)S(1)} copy(bf16[8,100,2048]{2,0,1:T(8,128)(2,1)} %param.11) | data formatting | bytes 6553600 | tf_op jit(solution)/shard_map/optimization_barrier | solution.py:397
  28.7 3.5 %shard_map.109 = bf16[100,11776]{1,0:T(8,128)(2,1)} custom-call(s32[338]{0:T(512)S(1)} %get-tuple-element.470.meta, bf16[8,100,2048]{2,1,0:T(8,128)(2,1)S(1)} %copy.66.refs_0_), custom_call_target="tpu_custom_call" | custom-call | flops 1 | bytes 1 | tf_op jit(solution)/shard_map/pallas_call | solution.py:113
  32.2 6.0 %collective-permute-start.8 = (bf16[100,11776]{1,0:T(8,128)(2,1)}, bf16[100,11776]{1,0:T(8,128)(2,1)}, u32[]{:S(2)}, u32[]{:S(2)}) collective-permute-start(bf16[100,11776]{1,0:T(8,128)(2,1)} %shard_map.109), channel_id=1, source_target_pairs={{0,1},{4,5},{8,9},{12,13},{16,17},{20,21},{24,25},{28,29}} | collective-permute-start | bytes 7065608 | tf_op jit(solution)/shard_map/ppermute | solution.py:366
  38.2 2.1 collective-permute-start.9
  42.9 13.9 %pmax.7 = s32[2]{0:T(128)S(1)} all-reduce(s32[2]{0:T(128)S(1)} %pad_add_fusion.3), channel_id=1, replica_groups=mesh['sub'=8,'grp'=4] {'sub'}, use_global_device_ids=true, to_apply=%region_0.0 | all-reduce | flops 2 | bytes 16 | tf_op jit(solution)/shard_map/pmax | solution.py:458
  57.6 17.6 %shard_map.107.refs_0_ = bf16[448,12032]{1,0:T(8,128)(2,1)} custom-call(s32[338]{0:T(512)S(1)} %pad_add_fusion.2.meta, s32[8]{0:T(128)S(1)} %copy-done.14, s32[8,24]{1,0:T(8,128)S(1)} %copy-done.12, s32[8,24]{1,0:T(8,128)S(1)} %copy-done.13, bf16[8,100,2048]{2,1,0:T(8,128)(2,1)} %copy-done, bf16[8,24,128,128]{3,2,1,0:T(8,128)(2,1)} %refs_2_.3, ...), custom_call_target="tpu_custom_call" | custom-call | flops 1 | bytes 1 | tf_op jit(solution)/shard_map/pallas_call | solution.py:180
  75.2 1.9 collective-permute-done.5.refs_3_
  79.2 17.6 %shard_map.108 = bf16[8,100,1280]{2,1,0:T(8,128)(2,1)} custom-call(s32[338]{0:T(512)S(1)} %pad_add_fusion.2.meta, bf16[448,12032]{1,0:T(8,128)(2,1)} %shard_map.107.refs_0_, bf16[100,12032]{1,0:T(8,128)(2,1)} %shard_map.105.refs_1_, bf16[100,12032]{1,0:T(8,128)(2,1)} %collective-permute-done.4.refs_2_, bf16[100,12032]{1,0:T(8,128)(2,1)} %collective-permute-done.5.refs_3_), custom_call_target="tpu_custom_call" | custom-call | flops 1 | bytes 1 | tf_op jit(solution)/shard_map/pallas_call | solution.py:289
  96.8 8.3 %all-to-all-start.3 = ((bf16[8,100,1280]{2,1,0:T(8,128)(2,1)}), bf16[8,100,1280]{2,1,0:T(8,128)(2,1)}, u32[]{:S(2)}, u32[]{:S(2)}) async-start(bf16[8,100,1280]{2,1,0:T(8,128)(2,1)} %shard_map.108), calls=%async_computation.3 | async-start | bytes 4259840 | tf_op jit(solution)/shard_map/all_to_all | solution.py:373
  105.2 18.3 %collective-permute-done.8 = bf16[100,11776]{1,0:T(8,128)(2,1)} collective-permute-done((bf16[100,11776]{1,0:T(8,128)(2,1)}, bf16[100,11776]{1,0:T(8,128)(2,1)}, u32[]{:S(2)}, u32[]{:S(2)}) %collective-permute-start.8) | collective-permute-done | bytes 2355232 | tf_op jit(solution)/shard_map/ppermute | solution.py:366
  123.5 18.8 %shard_map.110.refs_1_ = bf16[448,12032]{1,0:T(8,128)(2,1)} custom-call(s32[338]{0:T(512)S(1)} %pad_add_fusion.2.meta, s32[8]{0:T(128)S(1)} %copy-done.14, s32[8,24]{1,0:T(8,128)S(1)} %get-tuple-element.688.row, s32[8,24]{1,0:T(8,128)S(1)} %copy-done.13, bf16[1,100,11776]{2,1,0:T(8,128)(2,1)} %bitcast.19.refs_0_, bf16[1,100,11776]{2,1,0:T(8,128)(2,1)} %bitcast.20.refs_1_, ...), custom_call_target="tpu_custom_call" | custom-call | flops 24999999488 | bytes 1 | tf_op jit(solution)/shard_map/pallas_call | solution.py:180
  142.2 17.9 %shard_map.111 = (bf16[8,100,512]{2,1,0:T(8,128)(2,1)}, bf16[8,100,512]{2,1,0:T(8,128)(2,1)}) custom-call(s32[338]{0:T(512)S(1)} %pad_add_fusion.2.meta, bf16[448,12032]{1,0:T(8,128)(2,1)} %shard_map.107.refs_0_, bf16[448,12032]{1,0:T(8,128)(2,1)} %shard_map.110.refs_1_, bf16[100,12032]{1,0:T(8,128)(2,1)S(1)} %collective-permute-done.6.refs_2_, ...), custom_call_target="tpu_custom_call" | custom-call | flops 1 | bytes 1 | tf_op jit(solution)/shard_map/pallas_call | solution.py:289
  160.2 1.4 copy.68
  162.9 24.4 %all_to_all.48.second = bf16[8,100,512]{2,1,0:T(8,128)(2,1)} all-to-all(bf16[8,100,512]{2,1,0:T(8,128)(2,1)} %get-tuple-element.475), channel_id=1, replica_groups=mesh['sub'=8,'grp'=4] {'sub'}, dimensions={0} | all-to-all | bytes 1638400 | tf_op jit(solution)/shard_map/all_to_all | solution.py:373
  188.4 4.4 %all-to-all-start.5 = ((bf16[8,100,512]{2,1,0:T(8,128)(2,1)}), bf16[8,100,512]{2,1,0:T(8,128)(2,1)}, u32[]{:S(2)}, u32[]{:S(2)}) async-start(bf16[8,100,512]{2,1,0:T(8,128)(2,1)} %copy.69), calls=%async_computation.5 | async-start | bytes 1703936 | tf_op jit(solution)/shard_map/all_to_all | solution.py:373
  192.8 3.7 %copy.81 = bf16[8,100,2048]{2,1,0:T(8,128)(2,1)S(1)} copy(bf16[8,100,2048]{2,0,1:T(8,128)(2,1)} %param.11) | data formatting | bytes 6553600 | tf_op args[0]
  196.6 9.4 %all-to-all-done.5.third = bf16[8,100,512]{2,1,0:T(8,128)(2,1)} async-done(((bf16[8,100,512]{2,1,0:T(8,128)(2,1)}), bf16[8,100,512]{2,1,0:T(8,128)(2,1)}, u32[]{:S(2)}, u32[]{:S(2)}) %all-to-all-start.5) | async-done | bytes 819232 | tf_op jit(solution)/shard_map/all_to_all | solution.py:373
  206.0 6.7 %shard_map.112 = (f32[100,8,800]{2,1,0:T(8,128)}, f32[100,8,800]{2,1,0:T(8,128)}) custom-call(s32[1]{0:T(128)} %bitcast.17.place, bf16[8,100,1280]{2,1,0:T(8,128)(2,1)} %all-to-all-done.3.near, bf16[8,100,512]{2,1,0:T(8,128)(2,1)} %all_to_all.48.second, bf16[8,100,512]{2,1,0:T(8,128)(2,1)} %all-to-all-done.5.third), custom_call_target="tpu_custom_call" | custom-call | flops 1 | bytes 1 | tf_op jit(solution)/shard_map/pallas_call | solution.py:344
  (36 shorter events, 11.0 us)
Async XLA Ops:
  0.6 7.8 %copy-start.13 = (s32[8,24]{1,0:T(8,128)S(1)}, s32[8,24]{1,0:T(8,128)}, u32[]{:S(2)}) copy-start(s32[8,24]{1,0:T(8,128)} %col.3) | copy-start | bytes 2308
  0.6 7.7 %copy-start.14 = (s32[8]{0:T(128)S(1)}, s32[8]{0:T(128)}, u32[]{:S(2)}) copy-start(s32[8]{0:T(128)} %live.7) | copy-start | bytes 100
  4.4 10.3 %copy-start.5 = (bf16[8,100,2048]{2,1,0:T(8,128)(2,1)}, bf16[8,100,2048]{2,1,0:T(8,128)(2,1)S(1)}, u32[]{:S(2)}) copy-start(bf16[8,100,2048]{2,1,0:T(8,128)(2,1)S(1)} %copy.82.refs_1_) | copy-start | bytes 9830404
  5.3 5.5 %collective-permute-start.3 = (bf16[100,2048]{1,0:T(8,128)(2,1)}, bf16[100,2048]{1,0:T(8,128)(2,1)}, u32[]{:S(2)}, u32[]{:S(2)}) collective-permute-start(bf16[100,2048]{1,0:T(8,128)(2,1)} %slice_bitcast_fusion.6), channel_id=1, source_target_pairs={{0,4},{4,8},{8,12},{12,16},{16,20},{20,24},{24,28},{1,5},{5,9},{9,... | collective-permute-start | bytes 1228808 | tf_op jit(solution)/shard_map/ppermute | solution.py:366
  10.7 11.1 %copy-start.12 = (s32[8,24]{1,0:T(8,128)S(1)}, s32[8,24]{1,0:T(8,128)}, u32[]{:S(2)}) copy-start(s32[8,24]{1,0:T(8,128)} %row.1) | copy-start | bytes 2308
  14.7 60.5 %collective-permute-start.4 = (bf16[100,12032]{1,0:T(8,128)(2,1)}, bf16[100,12032]{1,0:T(8,128)(2,1)}, u32[]{:S(2)}, u32[]{:S(2)}) collective-permute-start(bf16[100,12032]{1,0:T(8,128)(2,1)} %shard_map.105.refs_1_), channel_id=1, source_target_pairs={{0,1},{1,2},{2,3},{4,5},{5,6},{6,7},{8,9},{9,10},{10,11},{12,13},{... | collective-permute-start | bytes 7219208 | tf_op jit(solution)/shard_map/ppermute | solution.py:366
  20.5 56.6 %collective-permute-start.5 = (bf16[100,12032]{1,0:T(8,128)(2,1)}, bf16[100,12032]{1,0:T(8,128)(2,1)}, u32[]{:S(2)}, u32[]{:S(2)}) collective-permute-start(bf16[100,12032]{1,0:T(8,128)(2,1)} %shard_map.105.refs_1_), channel_id=1, source_target_pairs={{1,0},{2,1},{3,2},{5,4},{6,5},{7,6},{9,8},{10,9},{11,10},{13,12},{... | collective-permute-start | bytes 7219208 | tf_op jit(solution)/shard_map/ppermute | solution.py:366
  28.7 3.5 %copy-start = (bf16[8,100,2048]{2,1,0:T(8,128)(2,1)}, bf16[8,100,2048]{2,1,0:T(8,128)(2,1)S(1)}, u32[]{:S(2)}) copy-start(bf16[8,100,2048]{2,1,0:T(8,128)(2,1)S(1)} %copy.66.refs_0_) | copy-start | bytes 9830404
  28.7 28.1 %copy-start.15 = (s32[2]{0:T(128)S(1)}, s32[2]{0:T(128)}, u32[]{:S(2)}) copy-start(s32[2]{0:T(128)} %constant.101) | copy-start | bytes 28
  28.7 28.1 %copy-start.16 = (s32[2]{0:T(128)S(1)}, s32[2]{0:T(128)}, u32[]{:S(2)}) copy-start(s32[2]{0:T(128)} %constant.96.clone) | copy-start | bytes 28
  32.2 91.2 %collective-permute-start.8 = (bf16[100,11776]{1,0:T(8,128)(2,1)}, bf16[100,11776]{1,0:T(8,128)(2,1)}, u32[]{:S(2)}, u32[]{:S(2)}) collective-permute-start(bf16[100,11776]{1,0:T(8,128)(2,1)} %shard_map.109), channel_id=1, source_target_pairs={{0,1},{4,5},{8,9},{12,13},{16,17},{20,21},{24,25},{28,29}} | collective-permute-start | bytes 7065608 | tf_op jit(solution)/shard_map/ppermute | solution.py:366
  38.2 85.3 %collective-permute-start.9 = (bf16[100,11776]{1,0:T(8,128)(2,1)}, bf16[100,11776]{1,0:T(8,128)(2,1)}, u32[]{:S(2)}, u32[]{:S(2)}) collective-permute-start(bf16[100,11776]{1,0:T(8,128)(2,1)} %shard_map.109), channel_id=1, source_target_pairs={{3,2},{7,6},{11,10},{15,14},{19,18},{23,22},{27,26},{31,30}} | collective-permute-start | bytes 7065608 | tf_op jit(solution)/shard_map/ppermute | solution.py:366
  77.1 65.1 %collective-permute-start.6 = (bf16[100,12032]{1,0:T(8,128)(2,1)}, bf16[100,12032]{1,0:T(8,128)(2,1)S(1)}, u32[]{:S(2)}, u32[]{:S(2)}) collective-permute-start(bf16[100,12032]{1,0:T(8,128)(2,1)} %collective-permute-done.4.refs_2_), channel_id=1, source_target_pairs={{1,2},{2,3},{5,6},{6,7},{9,10},{10,11},{13,14},{14,15},{17,18},{18... | collective-permute-start | bytes 7219208 | tf_op jit(solution)/shard_map/ppermute | solution.py:366
  77.9 64.3 %collective-permute-start.7 = (bf16[100,12032]{1,0:T(8,128)(2,1)}, bf16[100,12032]{1,0:T(8,128)(2,1)}, u32[]{:S(2)}, u32[]{:S(2)}) collective-permute-start(bf16[100,12032]{1,0:T(8,128)(2,1)} %collective-permute-done.5.refs_3_), channel_id=1, source_target_pairs={{2,1},{1,0},{6,5},{5,4},{10,9},{9,8},{14,13},{13,12},{18,17},{17,1... | collective-permute-start | bytes 7219208 | tf_op jit(solution)/shard_map/ppermute | solution.py:366
  96.8 45.4 %all-to-all-start.3 = ((bf16[8,100,1280]{2,1,0:T(8,128)(2,1)}), bf16[8,100,1280]{2,1,0:T(8,128)(2,1)}, u32[]{:S(2)}, u32[]{:S(2)}) async-start(bf16[8,100,1280]{2,1,0:T(8,128)(2,1)} %shard_map.108), calls=%async_computation.3 | async-start | bytes 4259840 | tf_op jit(solution)/shard_map/all_to_all | solution.py:373
  142.2 18.0 %copy-start.6 = (bf16[100,12032]{1,0:T(8,128)(2,1)}, bf16[100,12032]{1,0:T(8,128)(2,1)S(1)}, u32[]{:S(2)}) copy-start(bf16[100,12032]{1,0:T(8,128)(2,1)S(1)} %collective-permute-done.6.refs_2_) | copy-start | bytes 7219204
  161.6 25.7 %collective-permute-start.10 = (bf16[8,100,512]{2,0,1:T(8,128)(2,1)S(1)}, bf16[8,100,512]{2,0,1:T(8,128)(2,1)S(1)}, u32[]{:S(2)}, u32[]{:S(2)}) collective-permute-start(bf16[8,100,512]{2,0,1:T(8,128)(2,1)S(1)} %copy.68), channel_id=1, source_target_pairs={{1,0},{2,3},{5,4},{6,7},{9,8},{10,11},{13,12},{14,15},{17,16},{18,... | collective-permute-start | bytes 2457608 | tf_op jit(solution)/shard_map/ppermute | solution.py:383
  188.4 17.5 %all-to-all-start.5 = ((bf16[8,100,512]{2,1,0:T(8,128)(2,1)}), bf16[8,100,512]{2,1,0:T(8,128)(2,1)}, u32[]{:S(2)}, u32[]{:S(2)}) async-start(bf16[8,100,512]{2,1,0:T(8,128)(2,1)} %copy.69), calls=%async_computation.5 | async-start | bytes 1703936 | tf_op jit(solution)/shard_map/all_to_all | solution.py:373
